TPU v7x, 32 devices: a whole 2x2x4 slice. The times are simulated.
32 devices in a mesh: dp: 8 (over y, x, core), tp: 4 (over z).
Axes of the slice: x: 2, y: 2, z: 4, core: 2. Of those that a mesh axis runs over, the one named last changes fastest.
Arguments:
- tokens: bfloat16 [32, 1024, 768], P('dp', 'tp'), may hold values from -6 to 6
- lengths: int32 [32], P('dp'), may hold values from 64 to 1024, as said below
- w_qkv: bfloat16 [3, 768, 768], P(None, 'dp', 'tp'), may hold values from -0.21875 to 0.21875
- w_out: bfloat16 [768, 768], P('tp', 'dp'), may hold values from -1.75 to 1.75
- w_gate_up: bfloat16 [2, 768, 2048], P(None, 'dp', 'tp'), may hold values from -0.21875 to 0.21875
- w_down: bfloat16 [2048, 768], P('tp', 'dp'), may hold values from -0.1875 to 0.1875
- gains: float32 [2, 768], P(None, ('dp', 'tp')), may hold values from 0.5 to 1.5
- cotangent: bfloat16 [32, 1024, 768], P('dp', 'tp'), may hold values from -6 to 6
Outputs:
- layer_out: bfloat16 [32, 1024, 768], P('dp', 'tp')
- grad_tokens: float32 [32, 1024, 768], P('dp', 'tp')
- grad_w_qkv: float32 [3, 768, 768], P(None, 'dp', 'tp')
- grad_w_out: float32 [768, 768], P('tp', 'dp')
- grad_w_gate_up: float32 [2, 768, 2048], P(None, 'dp', 'tp')
- grad_w_down: float32 [2048, 768], P('tp', 'dp')
- grad_gains: float32 [2, 768], P(None, ('dp', 'tp'))
Inputs may be any that keep to these rules, and one draw needn't show every extreme that they name: `lengths`: valid tokens of each sequence, counted from its start; among the 4 sequences of each index of dp at least one has all 1024.
All inputs are finite; a program needn't handle non-finite values.
Results may differ from a plain program's by a relative error of at most 0.023.
Values may be sent and summed in bfloat16 or wider, within the bound.
A program may use at most 192 MiB of HBM per device.

v0:
```python
import jax
import jax.numpy as jnp
from jax import lax
from jax.sharding import PartitionSpec as P

HEAD = 64


eps = 1e-06
masked_score = -1e30


def rope_tables(length, width):
    half = width // 2
    freqs = 10000.0 ** (-2.0 * jnp.arange(half, dtype=jnp.float32) / width)
    angles = jnp.arange(length, dtype=jnp.float32)[:, None] * freqs[None, :]
    angles = jnp.concatenate([angles, angles], axis=1)
    return (jnp.cos(angles), jnp.sin(angles))


def rotate(values, cosine, sine):
    half = values.shape[-1] // 2
    turned = jnp.concatenate([-values[..., half:], values[..., :half]], axis=-1)
    return values * cosine + turned * sine


def unrotate(grads, cosine, sine):
    half = grads.shape[-1] // 2
    scaled = grads * sine
    turned = jnp.concatenate([scaled[..., half:], -scaled[..., :half]], axis=-1)
    return grads * cosine + turned


def root_mean_square_forward(values, gain):
    scale = lax.rsqrt(jnp.mean(values * values, axis=-1, keepdims=True) + eps)
    unit = values * scale
    return (unit, scale, (unit * gain).astype(jnp.bfloat16))


def rms_backward(d_normed, unit, scale, gain):
    d_unit = d_normed * gain
    d_values = scale * (d_unit - unit * jnp.mean(d_unit * unit, axis=-1, keepdims=True))
    return (d_values, jnp.sum(d_normed * unit, axis=(0, 1)))


def allowed_keys(start, rows, seq_len, length):
    query_pos = start + jnp.arange(rows)
    key_pos = jnp.arange(seq_len)
    return (key_pos[None, :] <= query_pos[:, None]) & (key_pos[None, :] < length)


def block_scores(query_block, sequence_random_key, allowed, scale):
    scores = (
        jnp.einsum(
            "hqd,hkd->hqk", query_block, sequence_random_key, preferred_element_type=jnp.float32
        )
        * scale
    )
    return jnp.where(allowed[None], scores, masked_score)


def body(tokens, lengths, w_qkv, w_out, w_gate_up, w_down, gains, cotangent):
    batch, local_len, width = tokens.shape
    seq_len = local_len * lax.axis_size("tp")
    rows = min(512, seq_len)
    scale = HEAD ** (-0.5)
    full_gains = lax.all_gather(gains, ("dp", "tp"), axis=1, tiled=True)
    gain_attn = full_gains[0]
    gain_mlp = full_gains[1]
    wq_all, wo_all, wg_all, wd_all = (
        lax.all_gather(w_qkv, "dp", axis=1, tiled=True),
        lax.all_gather(w_out, "dp", axis=1, tiled=True),
        lax.all_gather(w_gate_up, "dp", axis=1, tiled=True),
        lax.all_gather(w_down, "dp", axis=1, tiled=True),
    )
    local_width = wq_all.shape[2]
    local_heads = local_width // HEAD
    inputs = tokens.astype(jnp.float32)
    positions = lax.axis_index("tp") * local_len + jnp.arange(local_len)
    valid = (positions[None, :] < lengths[:, None]).astype(jnp.float32)[..., None]
    cosine, sine = rope_tables(seq_len, HEAD)
    cosine = cosine[:, None, :]
    sine = sine[:, None, :]
    unit1, scale1, normed1 = root_mean_square_forward(inputs, gain_attn)
    tokens1 = lax.all_gather(normed1, "tp", axis=1, tiled=True)
    raw = jnp.einsum("bld,cde->cble", tokens1, wq_all, preferred_element_type=jnp.float32)
    raw = raw.reshape(3, batch, seq_len, local_heads, HEAD)
    queries = jnp.transpose(rotate(raw[0], cosine, sine).astype(jnp.bfloat16), (0, 2, 1, 3))
    keys = jnp.transpose(rotate(raw[1], cosine, sine).astype(jnp.bfloat16), (0, 2, 1, 3))
    values = jnp.transpose(raw[2].astype(jnp.bfloat16), (0, 2, 1, 3))

    def attend_sequence(item):
        query_seq, sequence_random_key, value_seq, length = item
        outputs = []
        totals = []
        for start in range(0, seq_len, rows):
            allowed = allowed_keys(start, rows, seq_len, length)
            scores = block_scores(
                query_seq[:, start : start + rows], sequence_random_key, allowed, scale
            )
            top = jnp.max(scores, axis=-1, keepdims=True)
            expo = jnp.exp(scores - top)
            total = jnp.sum(expo, axis=-1, keepdims=True)
            probs = (expo / total).astype(jnp.bfloat16)
            outputs.append(
                jnp.einsum("hqk,hkd->hqd", probs, value_seq, preferred_element_type=jnp.float32)
            )
            totals.append((top + jnp.log(total))[..., 0])
        return (
            jnp.concatenate(outputs, axis=1).astype(jnp.bfloat16),
            jnp.concatenate(totals, axis=1),
        )

    context, logged_totals = lax.map(attend_sequence, (queries, keys, values, lengths))
    context = jnp.transpose(context, (0, 2, 1, 3)).reshape(batch, seq_len, local_width)
    partial_out = jnp.einsum("ble,ed->bld", context, wo_all, preferred_element_type=jnp.float32)
    attn_out = lax.psum_scatter(
        partial_out.astype(jnp.bfloat16), "tp", scatter_dimension=1, tiled=True
    ).astype(jnp.float32)
    hidden = inputs + valid * attn_out
    unit2, scale2, normed2 = root_mean_square_forward(hidden, gain_mlp)
    tokens2 = lax.all_gather(normed2, "tp", axis=1, tiled=True)
    gate_up = jnp.einsum("bld,cdf->cblf", tokens2, wg_all, preferred_element_type=jnp.float32)
    gate = gate_up[0]
    up = gate_up[1]
    sigma = jax.nn.sigmoid(gate)
    swish = gate * sigma
    activated = (swish * up).astype(jnp.bfloat16)
    mlp_part = jnp.einsum("blf,fd->bld", activated, wd_all, preferred_element_type=jnp.float32)
    mlp_out = lax.psum_scatter(
        mlp_part.astype(jnp.bfloat16), "tp", scatter_dimension=1, tiled=True
    ).astype(jnp.float32)
    layer_out = (hidden + valid * mlp_out).astype(jnp.bfloat16)
    d_out = cotangent.astype(jnp.float32)
    d_mlp = (valid * d_out).astype(jnp.bfloat16)
    feedforward_gradient_total = lax.all_gather(d_mlp, "tp", axis=1, tiled=True)
    grad_down = jnp.einsum(
        "blf,bld->fd", activated, feedforward_gradient_total, preferred_element_type=jnp.float32
    )
    d_act = jnp.einsum(
        "bld,fd->blf", feedforward_gradient_total, wd_all, preferred_element_type=jnp.float32
    )
    d_gate = d_act * up * sigma * (1.0 + gate * (1.0 - sigma))
    d_up = d_act * swish
    d_gate_up = jnp.stack([d_gate, d_up]).astype(jnp.bfloat16)
    grad_gate_up = jnp.einsum(
        "bld,cblf->cdf", tokens2, d_gate_up, preferred_element_type=jnp.float32
    )
    d_norm2_part = jnp.einsum(
        "cblf,cdf->bld", d_gate_up, wg_all, preferred_element_type=jnp.float32
    )
    d_normed2 = lax.psum_scatter(
        d_norm2_part.astype(jnp.bfloat16), "tp", scatter_dimension=1, tiled=True
    ).astype(jnp.float32)
    d_hidden_norm, feedforward_gain_gradient = rms_backward(d_normed2, unit2, scale2, gain_mlp)
    d_hidden = d_out + d_hidden_norm
    d_attn = (valid * d_hidden).astype(jnp.bfloat16)
    d_attn_all = lax.all_gather(d_attn, "tp", axis=1, tiled=True)
    grad_out = jnp.einsum("ble,bld->ed", context, d_attn_all, preferred_element_type=jnp.float32)
    d_context = jnp.einsum(
        "bld,ed->ble", d_attn_all, wo_all, preferred_element_type=jnp.float32
    ).astype(jnp.bfloat16)
    d_context = jnp.transpose(d_context.reshape(batch, seq_len, local_heads, HEAD), (0, 2, 1, 3))

    def sequence_backward(item):
        query_seq, sequence_random_key, value_seq, total_seq, grad_seq, length = item
        query_grads = []
        key_grad = jnp.zeros(sequence_random_key.shape, jnp.float32)
        value_grad = jnp.zeros(value_seq.shape, jnp.float32)
        for start in range(0, seq_len, rows):
            query_block = query_seq[:, start : start + rows]
            grad_block = grad_seq[:, start : start + rows]
            allowed = allowed_keys(start, rows, seq_len, length)
            scores = block_scores(query_block, sequence_random_key, allowed, scale)
            probs = jnp.exp(scores - total_seq[:, start : start + rows, None])
            d_probs = jnp.einsum(
                "hqd,hkd->hqk", grad_block, value_seq, preferred_element_type=jnp.float32
            )
            delta = jnp.sum(probs * d_probs, axis=-1, keepdims=True)
            d_scores = (probs * (d_probs - delta)).astype(jnp.bfloat16)
            query_grads.append(
                jnp.einsum(
                    "hqk,hkd->hqd",
                    d_scores,
                    sequence_random_key,
                    preferred_element_type=jnp.float32,
                )
                * scale
            )
            key_grad = (
                key_grad
                + jnp.einsum(
                    "hqk,hqd->hkd", d_scores, query_block, preferred_element_type=jnp.float32
                )
                * scale
            )
            value_grad = value_grad + jnp.einsum(
                "hqk,hqd->hkd",
                probs.astype(jnp.bfloat16),
                grad_block,
                preferred_element_type=jnp.float32,
            )
        return (jnp.concatenate(query_grads, axis=1), key_grad, value_grad)

    d_queries, d_keys, d_values = lax.map(
        sequence_backward, (queries, keys, values, logged_totals, d_context, lengths)
    )
    d_qkv = (
        jnp.stack(
            [
                unrotate(jnp.transpose(d_queries, (0, 2, 1, 3)), cosine, sine),
                unrotate(jnp.transpose(d_keys, (0, 2, 1, 3)), cosine, sine),
                jnp.transpose(d_values, (0, 2, 1, 3)),
            ]
        )
        .reshape(3, batch, seq_len, local_width)
        .astype(jnp.bfloat16)
    )
    grad_qkv = jnp.einsum("bld,cble->cde", tokens1, d_qkv, preferred_element_type=jnp.float32)
    d_norm1_part = jnp.einsum("cble,cde->bld", d_qkv, wq_all, preferred_element_type=jnp.float32)
    d_normed1 = lax.psum_scatter(
        d_norm1_part.astype(jnp.bfloat16), "tp", scatter_dimension=1, tiled=True
    ).astype(jnp.float32)
    d_input_norm, grad_gain_attn = rms_backward(d_normed1, unit1, scale1, gain_attn)
    grad_tokens = d_hidden + d_input_norm
    g_qkv, g_out, g_gate_up, g_down = (
        lax.psum_scatter(grad_qkv, "dp", scatter_dimension=1, tiled=True),
        lax.psum_scatter(grad_out, "dp", scatter_dimension=1, tiled=True),
        lax.psum_scatter(grad_gate_up, "dp", scatter_dimension=1, tiled=True),
        lax.psum_scatter(grad_down, "dp", scatter_dimension=1, tiled=True),
    )
    g_gains = lax.psum_scatter(
        jnp.stack([grad_gain_attn, feedforward_gain_gradient]),
        ("dp", "tp"),
        scatter_dimension=1,
        tiled=True,
    )
    return (layer_out, grad_tokens, g_qkv, g_out, g_gate_up, g_down, g_gains)


def solution(mesh):
    return jax.shard_map(
        body,
        mesh=mesh,
        in_specs=(
            P("dp", "tp", None),
            P("dp"),
            P(None, "dp", "tp"),
            P("tp", "dp"),
            P(None, "dp", "tp"),
            P("tp", "dp"),
            P(None, ("dp", "tp")),
            P("dp", "tp", None),
        ),
        out_specs=(
            P("dp", "tp", None),
            P("dp", "tp", None),
            P(None, "dp", "tp"),
            P("tp", "dp"),
            P(None, "dp", "tp"),
            P("tp", "dp"),
            P(None, ("dp", "tp")),
        ),
        check_vma=False,
    )
```

profile of v0, /device:TPU:0, one launch (start us, length us, event | category | flops | bytes accessed | tf_op | source)
XLA Modules:
  0.0 1341.2 jit_solution(17312319162678896840)
XLA Ops:
  9.9 70.0 %all-gather = f32[32,24,2]{1,2,0:T(2,128)S(1)} all-gather(f32[1,24,2]{1,2,0:T(2,128)} %bitcast.278), channel_id=1, replica_groups=mesh['dp'=8,'tp'=4] {'dp','tp'}, dimensions={0}, use_global_device_ids=true | all-gather | bytes 6336 | tf_op jit(solution)/shard_map/all_gather | solution.py:67
  80.7 3.0 fusion.118
  84.0 12.2 all_gather.29
  97.2 9.8 all_gather.30
  108.7 86.8 %all-gather.7.cloned.1.call-done = bf16[4,1024,768]{2,1,0:T(8,128)(2,1)} async-done(((bf16[4,256,768]{2,1,0:T(8,128)(2,1)}), bf16[4,1024,768]{2,1,0:T(8,128)(2,1)}) %all-gather.7.cloned.1.call-update) | async-done | bytes 6291472 | tf_op jit(solution)/shard_map/all_gather | solution.py:85
  195.5 6.0 fusion.109
  207.3 56.9 %while.26 = (s32[]{:T(128)}, bf16[4,3,1024,64]{2,3,1,0:T(8,128)(2,1)}, f32[4,3,1024]{2,1,0:T(4,128)}, s32[4]{0:T(128)S(1)}, bf16[4,3,1024,64]{2,3,1,0:T(8,128)(2...) while((s32[]{:T(128)}, ...), condition=%wide.region_6.7_spmd, body=%wide.region_1.6_spmd.sunk | while | flops 846136832 | bytes 52308132 | solution.py:114
  211.9 3.5 fusion.209
  215.4 2.3 fusion.211
  217.7 2.3 fusion.210
  226.0 3.5 fusion.209
  229.6 2.3 fusion.211
  231.8 2.3 fusion.210
  240.2 3.5 fusion.209
  243.7 2.3 fusion.211
  246.0 2.3 fusion.210
  254.3 3.5 fusion.209
  257.8 2.3 fusion.211
  260.1 2.3 fusion.210
  264.2 6.5 convolution_convert_fusion.1
  271.5 108.4 %reduce-scatter.13.cloned.1.call-done = bf16[4,256,768]{2,1,0:T(8,128)(2,1)} async-done(((bf16[4,1024,768]{2,1,0:T(8,128)(2,1)}), bf16[4,256,768]{2,1,0:T(8,128)(2,1)}) %reduce-scatter.13.cloned.1.call-update) | async-done | bytes 1572880 | tf_op jit(solution)/shard_map/reduce_scatter | solution.py:117
  379.9 2.4 multiply_reduce_fusion.2
  382.3 2.6 fusion.116
  385.6 12.3 all_gather.33
  397.9 102.9 %all-gather.9.cloned.1.call-done = bf16[4,1024,768]{2,1,0:T(8,128)(2,1)} async-done(((bf16[4,256,768]{2,1,0:T(8,128)(2,1)}), bf16[4,1024,768]{2,1,0:T(8,128)(2,1)}) %all-gather.9.cloned.1.call-update) | async-done | bytes 6291472 | tf_op jit(solution)/shard_map/all_gather | solution.py:122
  500.8 12.9 convolution_bitcast_fusion
  513.6 102.5 %all-gather.13.cloned.1.call-done = bf16[4,1024,768]{2,1,0:T(8,128)(2,1)} async-done(((bf16[4,256,768]{2,1,0:T(8,128)(2,1)}), bf16[4,1024,768]{2,1,0:T(8,128)(2,1)}) %all-gather.13.cloned.1.call-update) | async-done | bytes 6291472 | tf_op jit(solution)/shard_map/all_gather | solution.py:136
  616.2 13.2 fusion.105
  629.4 1.9 copy-done.46
  632.8 8.7 bitcast_convert_fusion.1
  641.5 108.9 %reduce-scatter.17.cloned.1.call-done = bf16[4,256,768]{2,1,0:T(8,128)(2,1)} async-done(((bf16[4,1024,768]{2,1,0:T(8,128)(2,1)}), bf16[4,256,768]{2,1,0:T(8,128)(2,1)}) %reduce-scatter.17.cloned.1.call-update) | async-done | bytes 1572880 | tf_op jit(solution)/shard_map/reduce_scatter | solution.py:152
  750.4 4.5 fusion.117
  755.5 2.5 multiply_convert_fusion.5
  758.1 12.4 fusion.128
  770.5 5.7 copy.43
  776.4 97.8 %all-gather.15.cloned.1.call-done = bf16[4,1024,768]{2,1,0:T(8,128)(2,1)} async-done(((bf16[4,256,768]{2,1,0:T(8,128)(2,1)}), bf16[4,1024,768]{2,1,0:T(8,128)(2,1)}) %all-gather.15.cloned.1.call-update) | async-done | bytes 6291472 | tf_op jit(solution)/shard_map/all_gather | solution.py:158
  874.1 6.1 convolution_convert_fusion.2
  880.3 94.5 %while.27 = (s32[]{:T(128)}, f32[4,3,1024,64]{2,3,1,0:T(8,128)}, f32[4,3,1024,64]{2,3,1,0:T(8,128)}, bf16[4,3,1024,64]{2,3,1,0:T(8,128)(2,1)}, s32[4]{0:T(128)S(...) while((s32[]{:T(128)}, f32[4,3,1024,64]{2,3,1,0:T(8,128)}, ...), condition=%wide.region_15.16_spmd, body=%wide.region_12.15_spmd.sunk | while | flops 2063530496 | bytes 123857112 | solution.py:205
  889.8 2.5 multiply_reduce_fusion.5
  895.2 2.5 multiply_reduce_fusion.6
  913.4 2.5 multiply_reduce_fusion.5
  918.8 2.5 multiply_reduce_fusion.6
  936.9 2.5 multiply_reduce_fusion.5
  942.3 2.5 multiply_reduce_fusion.6
  960.4 2.5 multiply_reduce_fusion.5
  965.9 2.5 multiply_reduce_fusion.6
  974.8 3.7 multiply_bitcast_fusion.1
  978.9 2.0 fusion.155
  980.9 2.1 copy-done.13
  983.0 3.7 convolution_bitcast_fusion.2
  986.8 5.6 fusion.126
  994.1 6.7 fusion.135
  1000.8 2.7 copy.58
  1003.5 4.8 reshape.346
  1008.5 11.3 bitcast_convert_fusion
  1020.9 8.2 convolution_convert_fusion
  1029.2 9.2 convolution_bitcast_fusion.1
  1043.9 19.9 %reduce-scatter.23.cloned.1.call-done = f32[96,576]{1,0:T(8,128)} async-done(((f32[768,576]{1,0:T(8,128)}), f32[96,576]{1,0:T(8,128)}) %reduce-scatter.23.cloned.1.call-update) | async-done | bytes 221200
  1065.7 110.9 %reduce-scatter.19.cloned.1.call-done = bf16[4,256,768]{2,1,0:T(8,128)(2,1)} async-done(((bf16[4,1024,768]{2,1,0:T(8,128)(2,1)}), bf16[4,256,768]{2,1,0:T(8,128)(2,1)}) %reduce-scatter.19.cloned.1.call-update) | async-done | bytes 1572880 | tf_op jit(solution)/shard_map/reduce_scatter | solution.py:221
  1176.7 2.6 fusion.120
  1179.3 47.9 %all-reduce.1 = f32[2,768]{1,0:T(2,128)S(1)} all-reduce(f32[2,768]{1,0:T(2,128)S(1)} %pad_maximum_fusion.13), channel_id=10, replica_groups=mesh['dp'=8,'tp'=4] {'dp','tp'}, use_global_device_ids=true, to_apply=%region_24.25.clone | all-reduce | flops 1536 | bytes 12288
  1227.9 63.2 %reduce-scatter.15.cloned.1.call-done = bf16[4,256,768]{2,1,0:T(8,128)(2,1)} async-done(((bf16[4,1024,768]{2,1,0:T(8,128)(2,1)}), bf16[4,256,768]{2,1,0:T(8,128)(2,1)}) %reduce-scatter.15.cloned.1.call-update) | async-done | bytes 1572880 | tf_op jit(solution)/shard_map/reduce_scatter | solution.py:130
  1291.1 5.8 fusion.113
  1296.9 36.9 %reduce-scatter.21.cloned.1.call-done = f32[512,96]{0,1:T(8,128)} async-done(((f32[512,768]{0,1:T(8,128)}), f32[512,96]{0,1:T(8,128)}) %reduce-scatter.21.cloned.1.call-update) | async-done | bytes 196624 | tf_op jit(solution)/shard_map/reduce_scatter | solution.py:230
  (293 shorter events, 123.4 us)
Async XLA Ops:
  8.0 75.8 %copy-start.35 = (bf16[192,96]{1,0:T(8,128)(2,1)S(1)}, bf16[192,96]{1,0:T(8,128)(2,1)}, u32[]{:S(2)}) copy-start(bf16[192,96]{1,0:T(8,128)(2,1)} %param.15) | copy-start | bytes 110596
  8.0 75.9 %copy-start.24 = (bf16[3,96,192]{2,1,0:T(8,128)(2,1)S(1)}, bf16[3,96,192]{2,1,0:T(8,128)(2,1)}, u32[]{:S(2)}) copy-start(bf16[3,96,192]{2,1,0:T(8,128)(2,1)} %param.14) | copy-start | bytes 331780
  8.0 187.4 %all-gather.7.cloned.1.call-start = ((), (), s32[]{:S(2)}) async-start(), calls=%async_computation.7 | async-start | bytes 7864320 | tf_op jit(solution)/shard_map/all_gather | solution.py:85
  9.9 74.0 %copy-start.33 = (f32[4,256]{1,0:T(4,128)}, f32[4,256]{1,0:T(4,128)S(1)}, u32[]{:S(2)}) copy-start(f32[4,256]{1,0:T(4,128)S(1)} %add_rsqrt_fusion.1) | copy-start | bytes 12292
  80.7 3.2 copy-start.31
  83.7 296.2 %reduce-scatter.13.cloned.1.call-start = ((), (), s32[]{:S(2)}) async-start(), calls=%async_computation.8 | async-start | bytes 7864320 | tf_op jit(solution)/shard_map/reduce_scatter | solution.py:117
  96.3 105.2 %copy-start.11 = (bf16[3,768,192]{2,0,1:T(4,128)(2,1)}, bf16[3,768,192]{2,0,1:T(4,128)(2,1)S(1)}, u32[]{:S(2)}) copy-start(bf16[3,768,192]{2,0,1:T(4,128)(2,1)S(1)} %all_gather.29) | copy-start | bytes 2654212
  108.7 96.7 %copy-start.15 = (f32[1024,64]{0,1:T(8,128)}, f32[1024,64]{0,1:T(8,128)S(1)}, u32[]{:S(2)}) copy-start(f32[1024,64]{0,1:T(8,128)S(1)} %get-tuple-element.204) | copy-start | bytes 786436
  205.4 1.9 copy-start.40
  207.3 56.9 %copy-start.14 = (bf16[192,768]{0,1:T(8,128)(2,1)S(1)}, bf16[192,768]{0,1:T(8,128)(2,1)}, u32[]{:S(2)}) copy-start(bf16[192,768]{0,1:T(8,128)(2,1)} %all_gather.30) | copy-start | bytes 884740
  211.9 3.5 copy-start.6
  226.0 3.5 copy-start.6
  240.2 3.5 copy-start.6
  254.3 3.5 copy-start.6
  264.2 6.5 copy-start.5
  270.7 109.1 %copy-start = (bf16[4,256,768]{2,1,0:T(8,128)(2,1)S(1)}, bf16[4,256,768]{2,1,0:T(8,128)(2,1)}, u32[]{:S(2)}) copy-start(bf16[4,256,768]{2,1,0:T(8,128)(2,1)} %param.12) | copy-start | bytes 4718596
  270.7 111.5 %copy-start.27 = (f32[768]{0:T(1024)S(1)}, f32[768]{0:T(1024)}, u32[]{:S(2)}) copy-start(f32[768]{0:T(1024)} %get-tuple-element.130) | copy-start | bytes 9220
  270.8 127.1 %all-gather.11.cloned.1.call-start = ((), (), s32[]{:S(2)}) async-start(), calls=%async_computation.10 | async-start | bytes 1769472 | tf_op jit(solution)/shard_map/all_gather | solution.py:73
  271.3 229.4 %all-gather.9.cloned.1.call-start = ((), (), s32[]{:S(2)}) async-start(), calls=%async_computation.9 | async-start | bytes 7864320 | tf_op jit(solution)/shard_map/all_gather | solution.py:122
  271.5 483.5 %copy-start.25 = (f32[4,256]{1,0:T(4,128)}, f32[4,256]{1,0:T(4,128)S(1)}, u32[]{:S(2)}) copy-start(f32[4,256]{1,0:T(4,128)S(1)} %compare_convert_fusion) | copy-start | bytes 12292
  379.9 2.4 copy-start.2
  379.9 2.5 copy-start.8
  382.3 372.7 %copy-start.29 = (f32[4,256]{1,0:T(4,128)}, f32[4,256]{1,0:T(4,128)S(1)}, u32[]{:S(2)}) copy-start(f32[4,256]{1,0:T(4,128)S(1)} %add_rsqrt_fusion) | copy-start | bytes 12292
  384.9 231.2 %all-gather.13.cloned.1.call-start = ((), (), s32[]{:S(2)}) async-start(), calls=%async_computation.12 | async-start | bytes 7864320 | tf_op jit(solution)/shard_map/all_gather | solution.py:136
  385.5 364.9 %reduce-scatter.17.cloned.1.call-start = ((), (), s32[]{:S(2)}) async-start(), calls=%async_computation.13 | async-start | bytes 7864320 | tf_op jit(solution)/shard_map/reduce_scatter | solution.py:152
  616.2 16.6 %copy-start.41 = (bf16[2,768,512]{2,1,0:T(8,128)(2,1)S(1)}, bf16[2,768,512]{2,1,0:T(8,128)(2,1)}, u32[]{:S(2)}) copy-start(bf16[2,768,512]{2,1,0:T(8,128)(2,1)} %all-gather.11.cloned.1.call-done) | copy-start | bytes 4718596
  629.4 1.9 copy-start.46
  629.4 3.3 copy-start.47
  641.5 232.7 %all-gather.15.cloned.1.call-start = ((), (), s32[]{:S(2)}) async-start(), calls=%async_computation.14 | async-start | bytes 7864320 | tf_op jit(solution)/shard_map/all_gather | solution.py:158
  750.4 5.1 copy-start.3
  750.4 5.1 copy-start.9
  750.4 5.1 copy-start.10
  758.1 281.6 %all-reduce.4.cloned.1.call-start = ((), (), s32[]{:S(2)}) async-start(), calls=%async_computation.19 | async-start | bytes 6291456
  776.3 104.0 %copy-start.7 = (bf16[4,3,1024,64]{2,3,1,0:T(8,128)(2,1)S(1)}, bf16[4,3,1024,64]{2,3,1,0:T(8,128)(2,1)}, u32[]{:S(2)}) copy-start(bf16[4,3,1024,64]{2,3,1,0:T(8,128)(2,1)} %get-tuple-element.425) | copy-start | bytes 4718596
  776.3 265.9 %reduce-scatter.25.cloned.1.call-start = ((), (), s32[]{:S(2)}) async-start(), calls=%async_computation.18 | async-start | bytes 884736
  880.3 94.5 %copy-start.18 = (f32[1024,64]{0,1:T(8,128)S(1)}, f32[1024,64]{0,1:T(8,128)}, u32[]{:S(2)}) copy-start(f32[1024,64]{0,1:T(8,128)} %get-tuple-element.205) | copy-start | bytes 786436
  886.1 1.9 copy-start.42
  889.8 2.5 copy-start.43
  909.6 1.9 copy-start.42
  913.4 2.5 copy-start.43
  936.9 2.5 copy-start.43
  956.7 1.9 copy-start.42
  960.4 2.5 copy-start.43
  978.5 2.4 copy-start.19
  978.8 4.2 copy-start.13
  983.0 3.7 copy-start.16
  986.7 77.1 %reduce-scatter.23.cloned.1.call-start = ((), (), s32[]{:S(2)}) async-start(), calls=%async_computation.17 | async-start | bytes 2211840
  986.8 7.3 copy-start.44
  1003.5 4.9 copy-start.12
  1003.5 4.9 copy-start.21
  1008.4 168.3 %reduce-scatter.19.cloned.1.call-start = ((), (), s32[]{:S(2)}) async-start(), calls=%async_computation.15 | async-start | bytes 7864320 | tf_op jit(solution)/shard_map/reduce_scatter | solution.py:221
  1019.8 271.3 %reduce-scatter.15.cloned.1.call-start = ((), (), s32[]{:S(2)}) async-start(), calls=%async_computation.11 | async-start | bytes 7864320 | tf_op jit(solution)/shard_map/reduce_scatter | solution.py:130
  1029.1 9.3 copy-start.45
  1029.1 304.7 %reduce-scatter.21.cloned.1.call-start = ((), (), s32[]{:S(2)}) async-start(), calls=%async_computation.16 | async-start | bytes 1769472 | tf_op jit(solution)/shard_map/reduce_scatter | solution.py:230
  1038.4 3.3 copy-start.38
  1038.4 138.3 %copy-start.1 = (bf16[4,256,768]{2,1,0:T(8,128)(2,1)S(1)}, bf16[4,256,768]{2,1,0:T(8,128)(2,1)}, u32[]{:S(2)}) copy-start(bf16[4,256,768]{2,1,0:T(8,128)(2,1)} %param.12) | copy-start | bytes 4718596
  1038.4 138.3 %copy-start.32 = (f32[768]{0:T(1024)S(1)}, f32[768]{0:T(1024)}, u32[]{:S(2)}) copy-start(f32[768]{0:T(1024)} %copy-done.31) | copy-start | bytes 9220
  1039.6 251.5 %copy-start.4 = (bf16[4,256,768]{2,1,0:T(8,128)(2,1)S(1)}, bf16[4,256,768]{2,1,0:T(8,128)(2,1)}, u32[]{:S(2)}) copy-start(bf16[4,256,768]{2,1,0:T(8,128)(2,1)} %reduce-scatter.13.cloned.1.call-done) | copy-start | bytes 4718596
  1039.6 251.5 %copy-start.26 = (f32[4,256]{1,0:T(4,128)S(1)}, f32[4,256]{1,0:T(4,128)}, u32[]{:S(2)}) copy-start(f32[4,256]{1,0:T(4,128)} %copy-done.25) | copy-start | bytes 12292
  1039.7 251.4 %copy-start.28 = (f32[768]{0:T(1024)S(1)}, f32[768]{0:T(1024)}, u32[]{:S(2)}) copy-start(f32[768]{0:T(1024)} %get-tuple-element.130) | copy-start | bytes 9220
  1039.7 251.4 %copy-start.30 = (f32[4,256]{1,0:T(4,128)S(1)}, f32[4,256]{1,0:T(4,128)}, u32[]{:S(2)}) copy-start(f32[4,256]{1,0:T(4,128)} %copy-done.29) | copy-start | bytes 12292
  1065.7 113.6 %copy-start.39 = (f32[1,768]{1,0:T(1,128)S(1)}, f32[1,768]{1,0:T(1,128)}, u32[]{:S(2)}) copy-start(f32[1,768]{1,0:T(1,128)} %stack.41) | copy-start | bytes 9220
  1065.7 225.4 %copy-start.34 = (f32[4,256]{1,0:T(4,128)S(1)}, f32[4,256]{1,0:T(4,128)}, u32[]{:S(2)}) copy-start(f32[4,256]{1,0:T(4,128)} %copy-done.33) | copy-start | bytes 12292
  1065.7 225.4 %copy-start.37 = (f32[4,256]{1,0:T(4,128)S(1)}, f32[4,256]{1,0:T(4,128)}, u32[]{:S(2)}) copy-start(f32[4,256]{1,0:T(4,128)} %copy-done.36) | copy-start | bytes 12292
  (6 other events, 7.8 us)
Sparse Core Ops, SparseCore 0:
  83.8 111.6 all-gather.6
  270.9 108.9 reduce-scatter.12
  758.2 115.8 all-gather.14
Sparse Core Ops, SparseCore 1:
  273.1 23.7 all-gather.10
  385.0 115.7 all-gather.8
  502.8 113.4 all-gather.12
  641.5 108.8 reduce-scatter.16
  776.4 69.6 all-reduce.3
  986.8 33.1 reduce-scatter.24
  1023.6 40.2 reduce-scatter.22
  1066.0 110.6 reduce-scatter.18
  1178.8 112.2 reduce-scatter.14
  1295.0 38.8 reduce-scatter.20
where the time goes:
time: 1340 us
  waiting for transfers between devices  840 us (63%)
  matrix products  195 us (15%)
  blocking collectives  152 us (11%)
  other arithmetic  89.4 us (7%)
  local copies, waits for them, and re-layouts  46.4 us (3%)
  between operations  16.7 us (1%)
    reduce_scatter x1, waiting for transfers between devices, body(): lax.psum_scatter(d_norm1_part.astype(jnp.bfloat16), 'tp', scatter_dimensi...  111 us
    reduce_scatter x1, waiting for transfers between devices, body(): lax.psum_scatter(d_norm2_part.astype(jnp.bfloat16), 'tp', scatter_dimensi...  109 us
    reduce_scatter x1, waiting for transfers between devices, body(): lax.psum_scatter(partial_out.astype(jnp.bfloat16), 'tp', scatter_dimensio...  108 us
    all_gather x1, waiting for transfers between devices, body(): tokens2 = lax.all_gather(normed2, 'tp', axis=1, tiled=True)  103 us
    all_gather x1, waiting for transfers between devices, body(): feedforward_gradient_total = lax.all_gather(d_mlp, 'tp', axis=1, tiled=True)  103 us
    all_gather x1, waiting for transfers between devices, body(): d_attn_all = lax.all_gather(d_attn, 'tp', axis=1, tiled=True)  97.8 us
    all_gather x1, waiting for transfers between devices, body(): tokens1 = lax.all_gather(normed1, 'tp', axis=1, tiled=True)  86.8 us
    all_gather x1, blocking collectives, body(): full_gains = lax.all_gather(gains, ('dp', 'tp'), axis=1, tiled=True)  70 us
  transfers between devices with their start and end apart: 13, of which 10 were waited for; matrix products, arithmetic and copies ran while one was open for 16% of the time, Pallas kernels for 0%

commit v1 on v0

v1 whole, which is shorter than its diff:
```python
import jax
import jax.numpy as jnp
from jax import lax
from jax.sharding import PartitionSpec as P

HEAD = 64
EPS = 1e-06
MASKED = -1e30
F32 = jnp.float32
BF16 = jnp.bfloat16


def rope_tables(length, width):
    half = width // 2
    freqs = 10000.0 ** (-2.0 * jnp.arange(half, dtype=F32) / width)
    angles = jnp.arange(length, dtype=F32)[:, None] * freqs[None, :]
    angles = jnp.concatenate([angles, angles], axis=1)
    return jnp.cos(angles), jnp.sin(angles)


def rotate(values, cosine, sine):
    half = values.shape[-1] // 2
    turned = jnp.concatenate([-values[..., half:], values[..., :half]], axis=-1)
    return values * cosine + turned * sine


def unrotate(grads, cosine, sine):
    half = grads.shape[-1] // 2
    scaled = grads * sine
    turned = jnp.concatenate([scaled[..., half:], -scaled[..., :half]], axis=-1)
    return grads * cosine + turned


def dot(spec, a, b):
    return jnp.einsum(spec, a, b, preferred_element_type=F32)


def pack_weights(w_qkv, w_out, w_gate_up, w_down):
    attn = jnp.concatenate([w_qkv[0], w_qkv[1], w_qkv[2], w_out.T], axis=1)
    mlp = jnp.concatenate([w_gate_up[0], w_gate_up[1], w_down.T], axis=1)
    return attn, mlp


def unpack_grads(g_attn, g_mlp, hw, fw):
    g_qkv = jnp.stack([g_attn[:, i * hw : (i + 1) * hw] for i in range(3)])
    g_gate_up = jnp.stack([g_mlp[:, i * fw : (i + 1) * fw] for i in range(2)])
    return g_qkv, g_attn[:, 3 * hw :].T, g_gate_up, g_mlp[:, 2 * fw :].T


def gather_all(shard):
    cols = lax.all_gather(shard, "tp", axis=0)
    return lax.all_gather(cols, "dp", axis=1, tiled=True)


def scatter_all(full):
    rows = lax.psum_scatter(full, "dp", scatter_dimension=1, tiled=True)
    return lax.psum_scatter(rows, "tp", scatter_dimension=0, tiled=False)


def to_sequences(local):
    return lax.all_to_all(local, "tp", split_axis=0, concat_axis=1, tiled=True)


def to_positions(whole):
    return lax.all_to_all(whole, "tp", split_axis=1, concat_axis=0, tiled=True)


def compute(x16, cot16, lengths, w_attn, w_mlp, gains):
    n, t, d = x16.shape
    tp = w_attn.shape[0]
    hw, fw = w_attn.shape[2] // 4, w_mlp.shape[2] // 3
    heads = hw // HEAD
    scale = HEAD**-0.5
    x = x16.astype(F32)
    dout = cot16.astype(F32)
    pos = jnp.arange(t)
    valid = (pos[None, :] < lengths[:, None]).astype(F32)[..., None]
    cosine, sine = rope_tables(t, HEAD)
    r1 = lax.rsqrt(jnp.mean(x * x, axis=-1, keepdims=True) + EPS)
    xhat1 = x * r1
    n1 = (xhat1 * gains[0]).astype(BF16)
    raw = dot("ntd,zdcje->czjnte", n1, w_attn[:, :, : 3 * hw].reshape(tp, d, 3, heads, HEAD))
    q = rotate(raw[0], cosine, sine).astype(BF16)
    k = rotate(raw[1], cosine, sine).astype(BF16)
    v = raw[2].astype(BF16)
    ok = (pos[None, :] <= pos[:, None])[None] & (pos[None, None, :] < lengths[:, None, None])

    def attend(item):
        qh, kh, vh = item
        s = jnp.where(ok, dot("nqe,nke->nqk", qh, kh) * scale, MASKED)
        top = jnp.max(s, axis=-1, keepdims=True)
        e = jnp.exp(s - top)
        total = jnp.sum(e, axis=-1, keepdims=True)
        p = (e / total).astype(BF16)
        return dot("nqk,nke->nqe", p, vh).astype(BF16), top + jnp.log(total)

    flat = lambda a: a.reshape((tp * heads,) + a.shape[2:])
    ctx, lse = lax.map(attend, (flat(q), flat(k), flat(v)))
    ctx_t = jnp.transpose(ctx.reshape(tp, heads, n, t, HEAD), (2, 3, 0, 1, 4)).reshape(n, t, tp, hw)
    w_o = w_attn[:, :, 3 * hw :]
    attn = dot("ntze,zde->ntd", ctx_t, w_o)
    hidden = x + valid * attn
    r2 = lax.rsqrt(jnp.mean(hidden * hidden, axis=-1, keepdims=True) + EPS)
    xhat2 = hidden * r2
    n2 = (xhat2 * gains[1]).astype(BF16)
    dm = (valid * dout).astype(BF16)
    mlp = jnp.zeros((n, t, d), F32)
    dn2 = jnp.zeros((n, t, d), F32)
    g_mlp = []
    for z in range(tp):
        wg, wu, wd = (w_mlp[z, :, i * fw : (i + 1) * fw] for i in range(3))
        gate = dot("ntd,df->ntf", n2, wg)
        up = dot("ntd,df->ntf", n2, wu)
        s = jax.nn.sigmoid(gate)
        sw = gate * s
        act = (sw * up).astype(BF16)
        mlp += dot("ntf,df->ntd", act, wd)
        d_act = dot("ntd,df->ntf", dm, wd)
        dg = (d_act * up * s * (1.0 + gate * (1.0 - s))).astype(BF16)
        du = (d_act * sw).astype(BF16)
        dn2 += dot("ntf,df->ntd", dg, wg) + dot("ntf,df->ntd", du, wu)
        g_mlp.append(
            jnp.concatenate(
                [dot("ntd,ntf->df", n2, dg), dot("ntd,ntf->df", n2, du), dot("ntd,ntf->df", dm, act)], axis=1
            )
        )
    layer_out = (hidden + valid * mlp).astype(BF16)
    e2 = dn2 * gains[1]
    d_hidden = dout + r2 * (e2 - xhat2 * jnp.mean(e2 * xhat2, axis=-1, keepdims=True))
    gg2 = jnp.sum(dn2 * xhat2, axis=(0, 1))
    d_attn = (valid * d_hidden).astype(BF16)
    g_o = dot("ntd,ntze->zde", d_attn, ctx_t)
    d_ctx = dot("ntd,zdje->zjnte", d_attn, w_o.reshape(tp, d, heads, HEAD)).astype(BF16)

    def back(item):
        qh, kh, vh, l, g = item
        p = jnp.where(ok, jnp.exp(dot("nqe,nke->nqk", qh, kh) * scale - l), 0.0)
        dp = dot("nqe,nke->nqk", g, vh)
        delta = jnp.sum(p * dp, axis=-1, keepdims=True)
        ds = (p * (dp - delta)).astype(BF16)
        return (
            dot("nqk,nke->nqe", ds, kh) * scale,
            dot("nqk,nqe->nke", ds, qh) * scale,
            dot("nqk,nqe->nke", p.astype(BF16), g),
        )

    dq, dk, dv = lax.map(back, (flat(q), flat(k), flat(v), lse, flat(d_ctx)))
    d_qkv = jnp.stack([unrotate(dq, cosine, sine), unrotate(dk, cosine, sine), dv]).astype(BF16)
    d_qkv = jnp.transpose(d_qkv.reshape(3, tp, heads, n, t, HEAD), (3, 4, 1, 0, 2, 5)).reshape(n, t, tp, 3 * hw)
    g_qkv = dot("ntd,ntze->zde", n1, d_qkv)
    dn1 = dot("ntze,zde->ntd", d_qkv, w_attn[:, :, : 3 * hw])
    e1 = dn1 * gains[0]
    grad_x = d_hidden + r1 * (e1 - xhat1 * jnp.mean(e1 * xhat1, axis=-1, keepdims=True))
    gg1 = jnp.sum(dn1 * xhat1, axis=(0, 1))
    g_attn = jnp.concatenate([g_qkv, g_o], axis=2)
    return layer_out, grad_x, g_attn, jnp.stack(g_mlp), jnp.stack([gg1, gg2])


def body(tokens, lengths, w_qkv, w_out, w_gate_up, w_down, gains, cotangent):
    tp = lax.axis_size("tp")
    batch = tokens.shape[0]
    n = batch // tp
    hw, fw = w_qkv.shape[2], w_gate_up.shape[2]
    full_gains = lax.all_gather(gains, ("dp", "tp"), axis=1, tiled=True)
    attn, mlp = pack_weights(w_qkv, w_out, w_gate_up, w_down)
    x16 = to_sequences(tokens)
    w_attn = gather_all(attn)
    w_mlp = gather_all(mlp)
    cot16 = to_sequences(cotangent)
    own = lax.dynamic_slice_in_dim(lengths, lax.axis_index("tp") * n, n)
    layer_out, grad_x, g_attn, g_mlp, g_gains = compute(x16, cot16, own, w_attn, w_mlp, full_gains)
    out = to_positions(layer_out)
    gx = to_positions(grad_x.astype(BF16)).astype(F32)
    s_mlp = scatter_all(g_mlp)
    s_attn = scatter_all(g_attn)
    s_gains = lax.psum_scatter(g_gains, ("dp", "tp"), scatter_dimension=1, tiled=True)
    g_qkv, g_out, g_gate_up, g_down = unpack_grads(s_attn, s_mlp, hw, fw)
    return out, gx, g_qkv, g_out, g_gate_up, g_down, s_gains


def solution(mesh):
    act = P("dp", "tp", None)
    ins = (act, P("dp"), P(None, "dp", "tp"), P("tp", "dp"), P(None, "dp", "tp"), P("tp", "dp"), P(None, ("dp", "tp")), act)
    outs = (act, act, P(None, "dp", "tp"), P("tp", "dp"), P(None, "dp", "tp"), P("tp", "dp"), P(None, ("dp", "tp")))
    return jax.shard_map(body, mesh=mesh, in_specs=ins, out_specs=outs, check_vma=False)
```

time: 1340 us -> 1180 us (0.88)
  waiting for transfers between devices: 840 us -> 373 us
  matrix products: 195 us -> 298 us
  local copies, waits for them, and re-layouts: 46.4 us -> 141 us
  blocking collectives: 152 us -> 215 us
  other arithmetic: 89.4 us -> 112 us
    reduce_scatter x5 -> x2, waiting for transfers between devices: 428 us -> 0.01 us  [scatter_all(): return lax.psum_scatter(rows, 'tp', scatter_dimension=0, tiled=False)]
    all_gather x5 -> x3, waiting for transfers between devices: 390 us -> 0.02 us  [the longest x2 0.02 us: gather_all(): return lax.all_gather(cols, 'dp', axis=1, tiled=True)]
    unnamed x16 -> x7, waiting for transfers between devices: 21.2 us -> 337 us
    dot_general x68 -> x126, matrix products: 195 us -> 298 us  [dot(): return jnp.einsum(spec, a, b, preferred_element_type=F32)]
    all_to_all x0 -> x1, blocking collectives: none -> 43.4 us  [to_sequences(): return lax.all_to_all(local, 'tp', split_axis=0, concat_axis=1, tiled=True)]
    unnamed x102 -> x106, local copies, waits for them, and re-layouts: 23.5 us -> 59.2 us
    all_to_all x0 -> x3, waiting for transfers between devices: none -> 35.4 us  [the longest x2 35.3 us: to_positions(): return lax.all_to_all(whole, 'tp', split_axis=1, concat_axis=0, tiled=True)]
    all_gather x1, blocking collectives: 70 us -> 93.7 us  [body(): full_gains = lax.all_gather(gains, ('dp', 'tp'), axis=1, tiled=True)]
  transfers between devices with their start and end apart: 13 -> 9, of which waited for: 10 -> 2; matrix products, arithmetic and copies ran while one was open for 16% -> 20% of each run, Pallas kernels for 0% -> 0%
where the time goes in v1:
time: 1180 us; the launch traced here: 1170 us
  waiting for transfers between devices  373 us (32%)
  matrix products  298 us (25%)
  blocking collectives  215 us (18%)
  local copies, waits for them, and re-layouts  141 us (12%)
  other arithmetic  112 us (9%)
  between operations  15.9 us (1%)
  starting transfers between devices  13.5 us (1%)
    unnamed x7, waiting for transfers between devices  337 us
    dot_general x126, matrix products, dot(): return jnp.einsum(spec, a, b, preferred_element_type=F32)  298 us
    all_gather x1, blocking collectives, body(): full_gains = lax.all_gather(gains, ('dp', 'tp'), axis=1, tiled=True)  93.7 us
    unnamed x106, local copies, waits for them, and re-layouts  59.2 us
    unnamed x1, blocking collectives  53.8 us
    all_to_all x1, blocking collectives, to_sequences(): return lax.all_to_all(local, 'tp', split_axis=0, concat_axis=1, tiled=True)  43.4 us
    all_to_all x2, waiting for transfers between devices, to_positions(): return lax.all_to_all(whole, 'tp', split_axis=1, concat_axis=0, tiled=True)  35.3 us
    all_gather x1, blocking collectives, gather_all(): cols = lax.all_gather(shard, 'tp', axis=0)  24.4 us
  transfers between devices with their start and end apart: 9, of which 2 were waited for; matrix products, arithmetic and copies ran while one was open for 20% of the time, Pallas kernels for 0%

profile of v1, /device:TPU:0, one launch (start us, length us, event | category | flops | bytes accessed | tf_op | source)
XLA Modules:
  0.0 1169.3 jit_solution(13398452626680473700)
XLA Ops:
  11.9 24.4 %all-gather = bf16[384,768]{1,0:T(8,128)(2,1)S(1)} all-gather(bf16[96,768]{1,0:T(8,128)(2,1)S(1)} %pad_maximum_fusion.7), channel_id=2, replica_groups=mesh['dp'=8,'tp'=4] {'tp'}, dimensions={0}, use_global_device_ids=true | all-gather | bytes 737280 | tf_op jit(solution)/shard_map/all_gather | solution.py:51
  37.6 43.4 %all_to_all.19 = bf16[4,256,768]{2,1,0:T(8,128)(2,1)S(1)} all-to-all(bf16[4,256,768]{2,1,0:T(8,128)(2,1)S(1)} %copy-done.27), channel_id=1, replica_groups=mesh['dp'=8,'tp'=4] {'tp'}, dimensions={0} | all-to-all | bytes 3145728 | tf_op jit(solution)/shard_map/all_to_all | solution.py:61
  81.0 4.3 all-to-all-start.2
  85.5 93.7 %all-gather.2 = f32[32,24,2]{1,2,0:T(2,128)S(1)} all-gather(f32[1,24,2]{1,2,0:T(2,128)S(1)} %bitcast.425), channel_id=1, replica_groups=mesh['dp'=8,'tp'=4] {'dp','tp'}, dimensions={0}, use_global_device_ids=true | all-gather | bytes 6336 | tf_op jit(solution)/shard_map/all_gather | solution.py:164
  192.8 5.9 slice.160
  198.6 8.0 copy.260
  206.6 8.3 convolution_bitcast_fusion
  214.9 4.2 fusion.100
  219.1 3.3 slice.251
  223.4 3.1 fusion.60
  226.5 3.1 copy.198
  229.6 4.1 copy.199
  233.7 4.1 copy.200
  237.9 3.7 slice.169
  241.6 3.6 copy.261
  245.2 74.9 %while.28 = (s32[]{:T(128)}, bf16[12,1,1024,64]{2,3,1,0:T(8,128)(2,1)}, f32[12,1,1024,1]{2,3,1,0:T(1,128)S(1)}, bf16[12,1,1024,64]{3,2,1,0:T(8,128)(2,1)S(1)}, b...) while((s32[]{:T(128)}, ...), condition=%wide.region_4.5_spmd.clone, body=%wide.region_1.4_spmd.clone.sunk | while | flops 287374336 | bytes 13546593 | solution.py:98
  321.8 4.3 multiply_reduce_fusion.4
  327.7 2.8 fusion.93
  330.4 3.3 fusion.94
  333.7 2.8 multiply_convert_fusion.6
  343.1 2.9 multiply_convert_fusion.8
  352.6 2.9 multiply_convert_fusion.10
  362.0 2.8 multiply_convert_fusion.12
  375.7 2.7 fusion.76
  378.4 6.3 multiply_reduce_fusion.1
  384.7 5.0 multiply_convert_fusion.1
  389.7 2.9 convolution_bitcast_fusion.2
  392.6 2.6 convolution_convert_fusion
  395.1 156.3 %while.29 = (s32[]{:T(128)}, f32[12,1,1024,64]{2,3,1,0:T(8,128)}, f32[12,1,1024,64]{2,3,1,0:T(8,128)}, bf16[12,1,1024,64]{2,3,1,0:T(8,128)(2,1)}, bf16[12,1,1024...) while((s32[]{:T(128)}, f32[12,1,1024,64]{2,3,1,0:T(8,128)}, ...), condition=%wide.region_9.10_spmd.clone, body=%wide.region_7.9_spmd.clone.sunk | while | flops 682753024 | bytes 33843320 | solution.py:147
  396.9 3.2 multiply_reduce_fusion.7
  409.9 3.2 multiply_reduce_fusion.7
  422.8 3.2 multiply_reduce_fusion.7
  435.8 3.2 multiply_reduce_fusion.7
  448.8 3.2 multiply_reduce_fusion.7
  461.8 3.2 multiply_reduce_fusion.7
  474.8 3.2 multiply_reduce_fusion.7
  487.8 3.2 multiply_reduce_fusion.7
  500.8 3.2 multiply_reduce_fusion.7
  513.8 3.2 multiply_reduce_fusion.7
  526.8 3.2 multiply_reduce_fusion.7
  539.8 3.2 multiply_reduce_fusion.7
  551.5 3.7 broadcast_multiply_fusion.1
  560.6 4.0 fusion.61
  568.7 5.8 convolution_bitcast_fusion.1
  574.5 8.0 pad_maximum_fusion.1
  582.5 12.1 %copy.227 = f32[4,768,768]{2,0,1:T(4,128)} copy(f32[4,768,768]{1,2,0:T(8,128)} %pad_maximum_fusion.1) | data formatting | bytes 18874368 | tf_op jit(solution)/shard_map/concatenate | solution.py:155
  594.5 2.9 fusion.114
  607.6 6.7 pad_maximum_fusion
  614.3 22.8 %copy.229 = f32[4,768,1536]{2,0,1:T(4,128)} copy(f32[4,768,1536]{1,2,0:T(8,128)} %pad_maximum_fusion) | data formatting | bytes 37748736 | tf_op jit(solution)/shard_map/stack | solution.py:156
  639.0 337.3 %all-reduce.6.cloned.1.call-done = (f32[4,768,768]{2,0,1:T(4,128)}, f32[4,768,1536]{2,0,1:T(4,128)}) async-done(((f32[4,768,768]{2,0,1:T(4,128)}, f32[4,768,1536]{2,0,1:T(4,128)}), (f32[4,768,768]{2,0,1:T(4,128)}, f32[4,768,1536]{2,0,1:T(4,128)})) %all-reduce.6.cloned.1.call-update) | async-done | bytes 28311568
  986.0 3.7 fusion.73
  989.7 7.2 copy.206
  997.5 11.4 reduce.24
  1008.8 3.8 reshape.1031
  1012.6 4.6 all-to-all-start.1
  1021.4 7.6 fusion.63
  1030.9 7.2 copy.225
  1038.1 11.4 reduce.25
  1049.5 3.7 reshape.1029
  1053.3 35.3 %all-to-all-done.1 = bf16[4,2,98304]{2,1,0:T(2,128)(2,1)} async-done(((bf16[4,2,98304]{2,1,0:T(2,128)(2,1)}), bf16[4,2,98304]{2,1,0:T(2,128)(2,1)}, u32[]{:S(2)}, u32[]{:S(2)}) %all-to-all-start.1) | async-done | bytes 1572896 | tf_op jit(solution)/shard_map/all_to_all | solution.py:65
  1088.6 4.4 all-to-all-start.3
  1093.0 53.8 %all-reduce.2 = f32[2,768]{1,0:T(2,128)S(1)} all-reduce(f32[2,768]{1,0:T(2,128)S(1)} %pad_maximum_fusion.8), channel_id=8, replica_groups=mesh['dp'=8,'tp'=4] {'dp','tp'}, use_global_device_ids=true, to_apply=%region_17.18.clone | all-reduce | flops 1536 | bytes 12288
  1147.5 3.0 reshape.1032
  1151.9 3.1 reshape.1030
  (321 shorter events, 291.9 us)
Async XLA Ops:
  7.2 30.4 %copy-start.27 = (bf16[4,256,768]{2,1,0:T(8,128)(2,1)S(1)}, bf16[4,256,768]{2,1,0:T(8,128)(2,1)}, u32[]{:S(2)}) copy-start(bf16[4,256,768]{2,1,0:T(8,128)(2,1)} %param.12) | copy-start | bytes 4718596
  7.2 175.7 %all-gather.11.cloned.1.call-start = ((), (), s32[]{:S(2)}) async-start(), calls=%async_computation.10 | async-start | bytes 1474560 | tf_op jit(solution)/shard_map/all_gather | solution.py:51
  9.9 182.8 %all-gather.7.cloned.1.call-start = ((), (), s32[]{:S(2)}) async-start(), calls=%async_computation.6 | async-start | bytes 5308416 | tf_op jit(solution)/shard_map/all_gather | solution.py:52
  37.6 47.9 %copy-start.39 = (f32[2,24]{1,0:T(2,128)S(1)}, f32[2,24]{1,0:T(2,128)}, u32[]{:S(2)}) copy-start(f32[2,24]{1,0:T(2,128)} %param.18) | copy-start | bytes 580
  37.6 141.6 %copy-start.40 = (s32[4]{0:T(128)S(1)}, s32[4]{0:T(128)}, u32[]{:S(2)}) copy-start(s32[4]{0:T(128)} %param.13) | copy-start | bytes 52
  81.0 104.1 %copy-start = (bf16[4,256,768]{2,1,0:T(8,128)(2,1)}, bf16[4,256,768]{2,1,0:T(8,128)(2,1)S(1)}, u32[]{:S(2)}) copy-start(bf16[4,256,768]{2,1,0:T(8,128)(2,1)S(1)} %all_to_all.19) | copy-start | bytes 4718596
  81.0 105.1 %all-to-all-start.2 = ((bf16[4,256,768]{2,1,0:T(8,128)(2,1)}), bf16[4,256,768]{2,1,0:T(8,128)(2,1)}, u32[]{:S(2)}, u32[]{:S(2)}) async-start(bf16[4,256,768]{2,1,0:T(8,128)(2,1)} %param.19), calls=%async_computation.2 | async-start | bytes 3145728 | tf_op jit(solution)/shard_map/all_to_all | solution.py:61
  85.4 242.3 %all-gather.9.cloned.1.call-start = ((), (), s32[]{:S(2)}) async-start(), calls=%async_computation.7 | async-start | bytes 10616832 | tf_op jit(solution)/shard_map/all_gather | solution.py:52
  181.2 10.6 copy-start.35
  182.9 40.3 %copy-start.15 = (f32[1024,64]{0,1:T(8,128)}, f32[1024,64]{0,1:T(8,128)S(1)}, u32[]{:S(2)}) copy-start(f32[1024,64]{0,1:T(8,128)S(1)} %get-tuple-element.354) | copy-start | bytes 786436
  182.9 793.4 %all-reduce.6.cloned.1.call-start = ((), (), s32[]{:S(2)}) async-start(), calls=%async_computation.11 | async-start | bytes 56623104
  190.3 2.0 copy-start.1
  192.7 13.9 %copy-start.28 = (bf16[4,256,768]{2,1,0:T(8,128)(2,1)}, bf16[4,256,768]{2,1,0:T(8,128)(2,1)S(1)}, u32[]{:S(2)}) copy-start(bf16[4,256,768]{2,1,0:T(8,128)(2,1)S(1)} %multiply_convert_fusion.5) | copy-start | bytes 4718596
  222.5 0.9 copy-start.17
  320.1 1.7 copy-start.8
  327.7 6.0 copy-start.7
  330.4 3.3 copy-start.30
  333.7 2.8 copy-start.31
  384.7 5.0 copy-start.41
  389.7 2.9 copy-start.3
  389.7 2.9 copy-start.33
  395.1 156.3 %copy-start.18 = (f32[1024,64]{0,1:T(8,128)S(1)}, f32[1024,64]{0,1:T(8,128)}, u32[]{:S(2)}) copy-start(f32[1024,64]{0,1:T(8,128)} %get-tuple-element.355) | copy-start | bytes 786436
  555.2 3.5 copy-start.16
  556.7 3.0 copy-start.5
  556.7 4.0 copy-start.6
  564.7 4.0 copy-start.29
  566.5 2.2 copy-start.9
  594.5 2.9 copy-start.10
  594.5 2.9 copy-start.32
  597.4 1.2 copy-start.11
  598.6 1.2 copy-start.13
  599.7 1.4 copy-start.19
  599.8 1.9 copy-start.20
  601.6 1.4 copy-start.21
  601.6 1.9 copy-start.22
  603.5 1.4 copy-start.23
  603.5 1.9 copy-start.24
  605.4 1.4 copy-start.25
  605.4 1.9 copy-start.26
  637.1 0.7 copy-start.42
  637.2 519.7 %reduce-scatter.4.cloned.1.call-start = ((), (), s32[]{:S(2)}) async-start(), calls=%async_computation.8 | async-start | bytes 1474560 | tf_op jit(solution)/shard_map/reduce_scatter | solution.py:57
  979.0 2.6 copy-start.14
  981.5 2.2 copy-start.12
  983.8 2.3 copy-start.34
  1012.6 76.0 %all-to-all-start.1 = ((bf16[4,2,98304]{2,1,0:T(2,128)(2,1)}), bf16[4,2,98304]{2,1,0:T(2,128)(2,1)}, u32[]{:S(2)}, u32[]{:S(2)}) async-start(bf16[4,2,98304]{2,1,0:T(2,128)(2,1)} %reshape.1031), calls=%async_computation.1 | async-start | bytes 3145728 | tf_op jit(solution)/shard_map/all_to_all | solution.py:65
  1017.2 142.3 %reduce-scatter.6.cloned.1.call-start = ((), (), s32[]{:S(2)}) async-start(), calls=%async_computation.9 | async-start | bytes 2949120 | tf_op jit(solution)/shard_map/reduce_scatter | solution.py:57
  1019.0 2.2 copy-start.38
  1019.0 2.4 copy-start.2
  1019.0 2.4 copy-start.36
  1021.4 7.6 copy-start.4
  1049.5 43.4 %copy-start.37 = (f32[768]{0:T(1024)S(1)}, f32[768]{0:T(1024)}, u32[]{:S(2)}) copy-start(f32[768]{0:T(1024)} %get-tuple-element.266) | copy-start | bytes 9220
  1088.6 63.3 %all-to-all-start.3 = ((bf16[4,2,98304]{2,1,0:T(2,128)(2,1)}), bf16[4,2,98304]{2,1,0:T(2,128)(2,1)}, u32[]{:S(2)}, u32[]{:S(2)}) async-start(bf16[4,2,98304]{2,1,0:T(2,128)(2,1)} %reshape.1029), calls=%async_computation.3 | async-start | bytes 3145728 | tf_op jit(solution)/shard_map/all_to_all | solution.py:65
Sparse Core Ops, SparseCore 0:
  10.2 45.7 all-gather.10
  57.8 38.7 all-gather.6
  183.0 56.0 all-gather.8
  637.3 339.0 all-reduce.5
  979.1 29.2 reduce-scatter.3
  1021.3 69.6 reduce-scatter.5

commit v2 on v1

v2 whole, which is shorter than its diff:
```python
import numpy as np
import jax
import jax.numpy as jnp
from jax import lax
from jax.experimental import pallas as pl
from jax.experimental.pallas import tpu as pltpu
from jax.sharding import PartitionSpec as P

F32 = jnp.float32
BF16 = jnp.bfloat16
HEAD = 64
EPS = 1e-6
LOG2E = 1.4426950408889634
C2 = LOG2E * HEAD**-0.5
NEG = -1e30
BLK = 256


def dg(a, b, ca, cb):
    return lax.dot_general(a, b, (((ca,), (cb,)), ((), ())), preferred_element_type=F32)


def nn(a, b):
    return dg(a, b, 1, 0)


def nt(a, b):
    return dg(a, b, 1, 1)


def tn(a, b):
    return dg(a, b, 0, 0)


def rows_of(m):
    return pl.ds(pl.multiple_of(m * BLK, BLK), BLK)


def half_lane():
    return lax.broadcasted_iota(jnp.int32, (1, 128), 1) % HEAD < HEAD // 2


def head_lane(h):
    lane = lax.broadcasted_iota(jnp.int32, (1, 128), 1)
    return lane < HEAD if h == 0 else lane >= HEAD


def turned(v):
    return jnp.where(half_lane(), pltpu.roll(v, 96, 1), pltpu.roll(v, 32, 1))


def norm_rows(x, gain):
    r = lax.rsqrt(jnp.mean(x * x, axis=-1, keepdims=True) + EPS)
    return x * r, r


def qkv_stage(t, d, x_ref, gains_ref, wa_ref, cos_ref, sin_ref, n1_ref, q_ref, k_ref, v_ref):
    @pl.loop(0, t // BLK)
    def _(m):
        rs = rows_of(m)
        unit, _ = norm_rows(x_ref[rs, :].astype(F32), None)
        n1_ref[rs, :] = (unit * gains_ref[0:1, :]).astype(BF16)

    for c, out in enumerate((q_ref, k_ref, v_ref)):

        @pl.loop(0, d // 256)
        def _(j, c=c, out=out):
            cols = pl.ds(pl.multiple_of(c * d + j * 256, 256), 256)
            raw = nn(n1_ref[...], wa_ref[:, cols])
            for s in range(2):
                part = raw[:, s * 128 : (s + 1) * 128]
                if c < 2:
                    part = part * cos_ref[...] + turned(part) * sin_ref[...]
                out[:, pl.ds(pl.multiple_of(j * 256 + s * 128, 128), 128)] = part.astype(BF16)


def key_bias(t, length):
    pos = lax.broadcasted_iota(jnp.int32, (t, 1), 0)
    return jnp.where(pos < length, 0.0, NEG).astype(BF16)


def causal_block():
    key = lax.broadcasted_iota(jnp.int32, (BLK, BLK), 0)
    query = lax.broadcasted_iota(jnp.int32, (BLK, BLK), 1)
    return key <= query


def score_operands(h, qp, kp, bias):
    mine = head_lane(h)
    lane = lax.broadcasted_iota(jnp.int32, (1, 128), 1)
    spare = lane == (HEAD if h == 0 else 0)
    zero = jnp.zeros((), BF16)
    q_m = jnp.where(mine, qp, zero)
    k_m = jnp.where(mine, kp, zero)
    q_s = jnp.where(spare, jnp.ones((), BF16), q_m)
    k_s = jnp.where(spare, bias, k_m)
    return q_m, k_m, q_s, k_s


def mask_diag(s, i):
    if i == 0:
        return jnp.where(causal_block(), s, NEG)
    return jnp.concatenate([s[: i * BLK], jnp.where(causal_block(), s[i * BLK :], NEG)], axis=0)


def attend_stage(t, d, length, q_ref, k_ref, v_ref, ctxt_ref, lse_ref):
    bias = key_bias(t, length)

    @pl.loop(0, d // 128)
    def _(p):
        cols = pl.ds(pl.multiple_of(p * 128, 128), 128)
        qp, kp, vp = q_ref[:, cols], k_ref[:, cols], v_ref[:, cols]
        for h in range(2):
            _, _, q_s, k_s = score_operands(h, qp, kp, bias)
            for i in range(t // BLK):
                n = (i + 1) * BLK
                s = mask_diag(nt(k_s[:n], q_s[i * BLK : n]), i)
                top = jnp.max(s, axis=0, keepdims=True)
                e = jnp.exp2((s - top) * C2)
                total = jnp.sum(e, axis=0, keepdims=True)
                o = tn(vp[:n], e.astype(BF16))[h * HEAD : (h + 1) * HEAD] / total
                ctxt_ref[pl.ds(pl.multiple_of(p * 128 + h * HEAD, HEAD), HEAD), i * BLK : n] = o.astype(BF16)
                lse_ref[pl.ds(p * 2 + h, 1), i * BLK : n] = top * C2 + jnp.log2(total)


def out_stage(t, d, length, x_ref, wa_ref, ctxt_ref, hid_ref):
    @pl.loop(0, d // 256)
    def _(j):
        cols = pl.ds(pl.multiple_of(j * 256, 256), 256)
        out = dg(ctxt_ref[...], wa_ref[cols, 3 * d : 4 * d], 0, 1)
        pos = lax.broadcasted_iota(jnp.int32, (t, 1), 0)
        hid_ref[:, cols] = x_ref[:, cols].astype(F32) + jnp.where(pos < length, out, 0.0)


def k1(len_ref, x_ref, gains_ref, wa_ref, cos_ref, sin_ref, q_ref, k_ref, v_ref, ctxt_ref, lse_ref, hid_ref, n1_ref, stages=(1, 1, 1)):
    t, d = x_ref.shape
    length = len_ref[0]
    if stages[0]:
        qkv_stage(t, d, x_ref, gains_ref, wa_ref, cos_ref, sin_ref, n1_ref, q_ref, k_ref, v_ref)
    if stages[1]:
        attend_stage(t, d, length, q_ref, k_ref, v_ref, ctxt_ref, lse_ref)
    if stages[2]:
        out_stage(t, d, length, x_ref, wa_ref, ctxt_ref, hid_ref)


def token_mask(m, length):
    pos = m * BLK + lax.broadcasted_iota(jnp.int32, (BLK, 1), 0)
    return pos < length


def mlp_chunk(t, d, f, wm, gm, n2_ref, dm_ref, n2t_ref, dmt_ref, act_ref, dgu_ref, mlp_ref, dn2_ref, first):
    w = 256
    for j in range(f // w):
        lo, hi = j * w, (j + 1) * w
        gate = nn(n2_ref[...], wm[:, lo:hi])
        up = nn(n2_ref[...], wm[:, f + lo : f + hi])
        d_act = nn(dm_ref[...], wm[:, 2 * f + lo : 2 * f + hi])
        s = 1.0 / (1.0 + jnp.exp2(gate * (-LOG2E)))
        sw = gate * s
        act_ref[:, lo:hi] = (sw * up).astype(BF16)
        dgu_ref[:, lo:hi] = (d_act * up * (s + sw * (1.0 - s))).astype(BF16)
        dgu_ref[:, f + lo : f + hi] = (d_act * sw).astype(BF16)

    for j in range(d // 256):
        cols = slice(j * 256, (j + 1) * 256)
        a = nt(act_ref[...], wm[cols, 2 * f :])
        b = nt(dgu_ref[...], wm[cols, : 2 * f])
        if first:
            mlp_ref[:, cols] = a
            dn2_ref[:, cols] = b
        else:
            mlp_ref[:, cols] += a
            dn2_ref[:, cols] += b
    for j in range(2 * f // 256):
        cols = slice(j * 256, (j + 1) * 256)
        gm[:, cols] = nn(n2t_ref[...], dgu_ref[:, cols]).astype(BF16)
    for j in range(f // 256):
        cols = slice(j * 256, (j + 1) * 256)
        gm[:, 2 * f + j * 256 : 2 * f + (j + 1) * 256] = nn(dmt_ref[...], act_ref[:, cols]).astype(BF16)


def k2(len_ref, cot_ref, gains_ref, hid_ref, wm_ref, lo_ref, dh_ref, da_ref, gm_ref, gg_ref,
       n2_ref, dm_ref, n2t_ref, dmt_ref, act_ref, dgu_ref, mlp_ref, dn2_ref):
    t, d = cot_ref.shape
    tp, _, f3 = wm_ref.shape
    f = f3 // 3
    length = len_ref[0]

    @pl.loop(0, t // BLK)
    def _(m):
        rs = rows_of(m)
        unit, _ = norm_rows(hid_ref[rs, :], None)
        n2 = (unit * gains_ref[1:2, :]).astype(BF16)
        n2_ref[rs, :] = n2
        n2t_ref[:, rs] = n2.T
        dm = jnp.where(token_mask(m, length), cot_ref[rs, :], jnp.zeros((), BF16))
        dm_ref[rs, :] = dm
        dmt_ref[:, rs] = dm.T

    mlp_ref[...] = jnp.zeros_like(mlp_ref)
    dn2_ref[...] = jnp.zeros_like(dn2_ref)

    @pl.loop(0, tp)
    def _(z):
        mlp_chunk(t, d, f, wm_ref.at[z], gm_ref.at[z], n2_ref, dm_ref, n2t_ref, dmt_ref, act_ref, dgu_ref, mlp_ref, dn2_ref, False)

    gg_ref[...] = jnp.zeros_like(gg_ref)

    @pl.loop(0, t // BLK)
    def _(m):
        rs = rows_of(m)
        hid = hid_ref[rs, :]
        ok = token_mask(m, length)
        lo_ref[rs, :] = (hid + jnp.where(ok, mlp_ref[rs, :], 0.0)).astype(BF16)
        unit, r = norm_rows(hid, None)
        dn2 = dn2_ref[rs, :]
        gg_ref[...] += jnp.sum(dn2 * unit, axis=0, keepdims=True)
        e2 = dn2 * gains_ref[1:2, :]
        dh = cot_ref[rs, :].astype(F32) + r * (e2 - unit * jnp.mean(e2 * unit, axis=-1, keepdims=True))
        dh_ref[rs, :] = dh
        da_ref[rs, :] = jnp.where(ok, dh, 0.0).astype(BF16)


def k3(len_ref, x_ref, gains_ref, wa_ref, cos_ref, sin_ref, q_ref, k_ref, v_ref, ctxt_ref, lse_ref, dh_ref, da_ref,
       gx_ref, ga_ref, gg_ref, n1_ref, n1t_ref, dat_ref, dctx_ref, dlt_ref, dqkv_ref, dk_acc, dv_acc, dn1_ref, stages=(1, 1, 1)):
    t, d = x_ref.shape
    length = len_ref[0]

    if stages[0]:
        dat_ref[...] = da_ref[...].T

        @pl.loop(0, d // 256)
        def _(j):
            rs = pl.ds(pl.multiple_of(j * 256, 256), 256)
            cols = pl.ds(pl.multiple_of(3 * d + j * 256, 256), 256)
            ga_ref[:, cols] = nt(dat_ref[...], ctxt_ref[rs, :]).astype(BF16)
            dctx = nn(da_ref[...], wa_ref[:, cols]).astype(BF16)
            dctx_ref[:, rs] = dctx
            prod = dctx.T.astype(F32) * ctxt_ref[rs, :].astype(F32)
            for h in range(4):
                dlt_ref[pl.ds(j * 4 + h, 1), :] = jnp.sum(prod[h * HEAD : (h + 1) * HEAD], axis=0, keepdims=True)

    if stages[1]:
        bias = key_bias(t, length)

        @pl.loop(0, d // 128)
        def _(p):
            cols = pl.ds(pl.multiple_of(p * 128, 128), 128)
            qp, kp, vp, gp = q_ref[:, cols], k_ref[:, cols], v_ref[:, cols], dctx_ref[:, cols]
            dk_acc[...] = jnp.zeros_like(dk_acc)
            dv_acc[...] = jnp.zeros_like(dv_acc)
            ops = [score_operands(h, qp, kp, bias) for h in range(2)]
            for i in range(t // BLK):
                n = (i + 1) * BLK
                qs = slice(i * BLK, n)
                dq = None
                for h in range(2):
                    q_m, k_m, q_s, k_s = ops[h]
                    g_m = jnp.where(head_lane(h), gp[qs], jnp.zeros((), BF16))
                    s = mask_diag(nt(k_s[:n], q_s[qs]), i)
                    pr = jnp.exp2(s * C2 - lse_ref[pl.ds(p * 2 + h, 1), qs])
                    dp = nt(vp[:n], g_m)
                    ds = (pr * (dp - dlt_ref[pl.ds(p * 2 + h, 1), qs])).astype(BF16)
                    dv_acc[:n, :] += nn(pr.astype(BF16), g_m)
                    dk_acc[:n, :] += nn(ds, q_m[qs])
                    part = tn(ds, k_m[:n])
                    dq = part if dq is None else dq + part
                dq = dq * (HEAD**-0.5)
                dqkv_ref[qs, cols] = (dq * cos_ref[qs, :] - turned(dq) * sin_ref[qs, :]).astype(BF16)
            dk = dk_acc[...] * (HEAD**-0.5)
            dqkv_ref[:, pl.ds(pl.multiple_of(d + p * 128, 128), 128)] = (dk * cos_ref[...] - turned(dk) * sin_ref[...]).astype(BF16)
            dqkv_ref[:, pl.ds(pl.multiple_of(2 * d + p * 128, 128), 128)] = dv_acc[...].astype(BF16)

    if stages[2]:
        @pl.loop(0, t // BLK)
        def _(m):
            rs = rows_of(m)
            unit, _ = norm_rows(x_ref[rs, :].astype(F32), None)
            n1t_ref[:, rs] = (unit * gains_ref[0:1, :]).astype(BF16).T

        @pl.loop(0, 3 * d // 256)
        def _(j):
            cols = pl.ds(pl.multiple_of(j * 256, 256), 256)
            ga_ref[:, cols] = nn(n1t_ref[...], dqkv_ref[:, cols]).astype(BF16)

        @pl.loop(0, d // 256)
        def _(j):
            cols = pl.ds(pl.multiple_of(j * 256, 256), 256)
            dn1_ref[:, cols] = nt(dqkv_ref[...], wa_ref[cols, : 3 * d])

        gg_ref[...] = jnp.zeros_like(gg_ref)

        @pl.loop(0, t // BLK)
        def _(m):
            rs = rows_of(m)
            unit, r = norm_rows(x_ref[rs, :].astype(F32), None)
            dn1 = dn1_ref[rs, :]
            gg_ref[...] += jnp.sum(dn1 * unit, axis=0, keepdims=True)
            e1 = dn1 * gains_ref[0:1, :]
            gx_ref[rs, :] = (dh_ref[rs, :] + r * (e1 - unit * jnp.mean(e1 * unit, axis=-1, keepdims=True))).astype(BF16)


def rope_np(t):
    half = HEAD // 2
    freqs = np.float32(10000.0) ** (np.float32(-2.0) * np.arange(half, dtype=np.float32) / np.float32(HEAD))
    ang = np.arange(t, dtype=np.float32)[:, None] * freqs[None, :].astype(np.float32)
    c, s = np.cos(ang), np.sin(ang)
    return np.concatenate([c, c, c, c], 1).astype(np.float32), np.concatenate([-s, s, -s, s], 1).astype(np.float32)


VM = pl.BlockSpec(memory_space=pltpu.VMEM)
SM = pl.BlockSpec(memory_space=pltpu.SMEM)


def call(kernel, ins, outs, scratch):
    return pl.pallas_call(
        kernel,
        out_shape=[jax.ShapeDtypeStruct(s, dt) for s, dt in outs],
        in_specs=[SM] + [VM] * (len(ins) - 1),
        out_specs=[VM] * len(outs),
        scratch_shapes=[pltpu.VMEM(s, dt) for s, dt in scratch],
        compiler_params=pltpu.CompilerParams(vmem_limit_bytes=60 * 2**20),
    )(*ins)


def one_sequence(length, x, cot, gains, wa, wm, cosine, sine):
    t, d = x.shape
    f = wm.shape[2] // 3
    heads = -(-d // HEAD // 8) * 8
    td, dt = ((t, d), BF16), ((d, t), BF16)
    q, k, v, ctxt, lse, hid = call(
        k1, (length, x, gains, wa, cosine, sine), (td, td, td, dt, ((heads, t), F32), ((t, d), F32)), (td,)
    )
    lo, dh, da, gm, gg2 = call(
        k2,
        (length, cot, gains, hid, wm),
        (td, ((t, d), F32), td, (wm.shape, BF16), ((1, d), F32)),
        (td, td, dt, dt, ((t, f), BF16), ((t, 2 * f), BF16), ((t, d), F32), ((t, d), F32)),
    )
    gx, ga, gg1 = call(
        k3,
        (length, x, gains, wa, cosine, sine, q, k, v, ctxt, lse, dh, da),
        (td, ((d, 4 * d), BF16), ((1, d), F32)),
        (td, dt, dt, td, ((heads, t), F32), ((t, 3 * d), BF16), ((t, 128), F32), ((t, 128), F32), ((t, d), F32)),
    )
    return lo, gx, ga, gm, jnp.concatenate([gg1, gg2])


def pack_weights(w_qkv, w_out, w_gate_up, w_down):
    attn = jnp.stack([w_qkv[0], w_qkv[1], w_qkv[2], w_out.T], axis=1)
    mlp = jnp.concatenate([w_gate_up[0], w_gate_up[1], w_down.T], axis=1)
    return attn, mlp


def unpack_grads(g_attn, g_mlp, fw):
    g_qkv = jnp.transpose(g_attn[:, :3], (1, 0, 2))
    g_gate_up = jnp.stack([g_mlp[:, i * fw : (i + 1) * fw] for i in range(2)])
    return g_qkv, g_attn[:, 3].T, g_gate_up, g_mlp[:, 2 * fw :].T


def to_sequences(local):
    return lax.all_to_all(local, "tp", split_axis=0, concat_axis=1, tiled=True)


def to_positions(whole):
    return lax.all_to_all(whole, "tp", split_axis=1, concat_axis=0, tiled=True)


def body(tokens, lengths, w_qkv, w_out, w_gate_up, w_down, gains, cotangent):
    tp = lax.axis_size("tp")
    batch, part, d = tokens.shape
    n, t = batch // tp, part * tp
    fw = w_gate_up.shape[2]
    cosine, sine = map(jnp.asarray, rope_np(t))
    full_gains = lax.all_gather(gains, ("dp", "tp"), axis=1, tiled=True)
    full_gains = jnp.pad(full_gains, ((0, 6), (0, 0)))
    attn, mlp = pack_weights(w_qkv, w_out, w_gate_up, w_down)
    x16 = to_sequences(tokens)
    wa = lax.all_gather(attn, "tp", axis=2, tiled=True).reshape(attn.shape[0], 4 * d)
    wa = lax.all_gather(wa, "dp", axis=0, tiled=True)
    wm = lax.all_gather(lax.all_gather(mlp, "tp", axis=0), "dp", axis=1, tiled=True)
    cot16 = to_sequences(cotangent)
    own = lax.dynamic_slice_in_dim(lengths, lax.axis_index("tp") * n, n)
    los, gxs, ga, gm, gg = [], [], 0.0, 0.0, 0.0
    for i in range(n):
        lo, gx, a, m, g = one_sequence(own[i : i + 1], x16[i], cot16[i], full_gains, wa, wm, cosine, sine)
        los.append(lo)
        gxs.append(gx)
        ga, gm, gg = ga + a.astype(F32), gm + m.astype(F32), gg + g
    out = to_positions(jnp.stack(los))
    gx = to_positions(jnp.stack(gxs)).astype(F32)
    s_mlp = lax.psum_scatter(lax.psum_scatter(gm, "dp", scatter_dimension=1, tiled=True), "tp", scatter_dimension=0)
    s_attn = lax.psum_scatter(ga, "dp", scatter_dimension=0, tiled=True)
    s_attn = lax.psum_scatter(s_attn.reshape(-1, 4, d), "tp", scatter_dimension=2, tiled=True)
    s_gains = lax.psum_scatter(gg, ("dp", "tp"), scatter_dimension=1, tiled=True)
    return (out, gx) + unpack_grads(s_attn, s_mlp, fw) + (s_gains,)


def solution(mesh):
    act = P("dp", "tp", None)
    cols, rows, gain = P(None, "dp", "tp"), P("tp", "dp"), P(None, ("dp", "tp"))
    return jax.shard_map(
        body,
        mesh=mesh,
        in_specs=(act, P("dp"), cols, rows, cols, rows, gain, act),
        out_specs=(act, act, cols, rows, cols, rows, gain),
        check_vma=False,
    )
```

time: 1180 us -> 679 us (0.58)
  matrix products: 298 us -> 0 us
  waiting for transfers between devices: 373 us -> 161 us
  Pallas kernels: 0 us -> 132 us
  local copies, waits for them, and re-layouts: 141 us -> 39.6 us
  other arithmetic: 112 us -> 49.1 us
  blocking collectives: 215 us -> 254 us
    unnamed x7, waiting for transfers between devices: 337 us -> 0.11 us
    dot_general x126 -> x0, matrix products: 298 us -> none  [dot(): return jnp.einsum(spec, a, b, preferred_element_type=F32)]
    reduce_scatter x2 -> x4, waiting for transfers between devices: 0.01 us -> 151 us  [the longest x1 102 us: body(): lax.psum_scatter(gm, 'dp', scatter_dimension=1, tiled=True)]
    pallas_call x0 -> x3, Pallas kernels: none -> 132 us  [call(): pl.pallas_call(kernel, out_shape=[jax.ShapeDtypeStruct(s, dt) for s, dt i...]
    unnamed x106 -> x27, local copies, waits for them, and re-layouts: 59.2 us -> 20.6 us
    unnamed x1, blocking collectives: 53.8 us -> 91.5 us
    all_to_all x2, waiting for transfers between devices: 35.3 us -> 0.01 us  [to_positions(): return lax.all_to_all(whole, 'tp', split_axis=1, concat_axis=0, tiled=True)]
    reduce_sum x13 -> x0, other arithmetic: 23.5 us -> none  [the longest x12 23.1 us: attend(): total = jnp.sum(e, axis=-1, keepdims=True)]
  transfers between devices with their start and end apart: 9 -> 10, of which waited for: 2 -> 3; matrix products, arithmetic and copies ran while one was open for 20% -> 11% of each run, Pallas kernels for 0% -> 5%
where the time goes in v2:
time: 679 us; the launch traced here: 672 us
  blocking collectives  254 us (37%)
  waiting for transfers between devices  161 us (24%)
  Pallas kernels  132 us (19%)
  other arithmetic  49.1 us (7%)
  local copies, waits for them, and re-layouts  39.6 us (6%)
  starting transfers between devices  22 us (3%)
  between operations  14.7 us (2%)
    pallas_call x3, Pallas kernels, call(): pl.pallas_call(kernel, out_shape=[jax.ShapeDtypeStruct(s, dt) for s, dt i...  132 us
    reduce_scatter x1, waiting for transfers between devices, body(): lax.psum_scatter(gm, 'dp', scatter_dimension=1, tiled=True)  102 us
    all_gather x1, blocking collectives, body(): full_gains = lax.all_gather(gains, ('dp', 'tp'), axis=1, tiled=True)  93.6 us
    unnamed x1, blocking collectives  91.5 us
    reduce_scatter x1, waiting for transfers between devices, body(): s_attn = lax.psum_scatter(ga, 'dp', scatter_dimension=0, tiled=True)  48.9 us
    all_to_all x1, blocking collectives, to_sequences(): return lax.all_to_all(local, 'tp', split_axis=0, concat_axis=1, tiled=True)  40.6 us
    all_gather x1, blocking collectives, body(): lax.all_gather(attn, 'tp', axis=2, tiled=True).reshape(attn.shape[0], 4 * d)  27.9 us
    convert_element_type x2, other arithmetic, body(): ga, gm, gg = (ga + a.astype(F32), gm + m.astype(F32), gg + g)  23.4 us
  transfers between devices with their start and end apart: 10, of which 3 were waited for; matrix products, arithmetic and copies ran while one was open for 11% of the time, Pallas kernels for 5%

profile of v2, /device:TPU:0, one launch (start us, length us, event | category | flops | bytes accessed | tf_op | source)
XLA Modules:
  0.0 671.7 jit_solution(10799828059824250234)
XLA Ops:
  7.2 0.0 copy-start.2
  7.2 0.0 all-gather.10.cloned.1.call-start
  7.2 1.0 slice_bitcast_fusion.6
  8.2 1.6 pad_maximum_fusion.1
  9.8 0.0 all-gather.10.cloned.1.call-update
  9.8 0.0 all-gather.6.cloned.1.call-start
  9.9 0.9 fusion
  10.7 0.1 copy.55
  10.9 0.1 copy.56
  11.0 0.1 copy.57
  11.1 0.0 copy-done.2
  11.1 0.1 pad_maximum_fusion.2
  11.2 27.9 %all_gather.19 = bf16[96,4,768]{0,2,1:T(8,128)(2,1)S(1)} all-gather(bf16[96,4,192]{0,2,1:T(8,128)(2,1)S(1)} %pad_maximum_fusion.2), channel_id=1, replica_groups=mesh['dp'=8,'tp'=4] {'tp'}, dimensions={2}, use_global_device_ids=true | all-gather | bytes 737280 | tf_op jit(solution)/shard_map/all_gather | solution.py:379
  39.1 1.1 copy.51
  40.2 0.0 all-gather.6.cloned.1.call-update
  40.2 0.0 all-gather.8.cloned.1.call-start
  40.2 9.2 %all-gather.10.cloned.1.call-done = bf16[384,1536]{1,0:T(8,128)(2,1)} async-done(((bf16[96,1536]{1,0:T(8,128)(2,1)}), bf16[384,1536]{1,0:T(8,128)(2,1)}) %all-gather.10.cloned.1.call-update) | async-done | bytes 1179664 | tf_op jit(solution)/shard_map/all_gather | solution.py:381
  49.5 0.0 all-gather.8.cloned.1.call-update
  49.5 40.6 %all_to_all.19 = bf16[4,256,768]{2,1,0:T(8,128)(2,1)} all-to-all(bf16[4,256,768]{2,1,0:T(8,128)(2,1)S(1)} %copy-done.1), channel_id=1, replica_groups=mesh['dp'=8,'tp'=4] {'tp'}, dimensions={0} | all-to-all | bytes 3145728 | tf_op jit(solution)/shard_map/all_to_all | solution.py:362
  90.2 3.7 all-to-all-start
  93.9 0.0 reduce-scatter.6.cloned.1.call-start
  93.9 93.6 %all-gather.1 = f32[32,24,2]{1,2,0:T(2,128)S(1)} all-gather(f32[1,24,2]{1,2,0:T(2,128)S(1)} %bitcast.70), channel_id=1, replica_groups=mesh['dp'=8,'tp'=4] {'dp','tp'}, dimensions={0}, use_global_device_ids=true | all-gather | bytes 6336 | tf_op jit(solution)/shard_map/all_gather | solution.py:375
  187.5 0.1 reshape.41
  187.6 0.6 dynamic_slice.3.len_ref
  188.2 0.6 pad.4.gains_ref
  188.8 36.8 %shard_map.153 = (bf16[1024,768]{1,0:T(8,128)(2,1)}, bf16[1024,768]{1,0:T(8,128)(2,1)}, bf16[1024,768]{1,0:T(8,128)(2,1)}, bf16[768,1024]{1,0:T(8,128)(2,1)}, f32[16,1024]{1,0:T(8,128)}, /*index=5*/f32[1024,768]{1,0:T(8,128)}) custom-call(s32[1]{0:T(128)} %dynamic_slice.3.len_ref, bf16[1024,768]{1,0:T(8,128)(2,1)} %bitcast.49, f32[8,768]{1,0:T(8,128)} %pad.4.gains_ref, ...), custom_call_target="tpu_custom_call" | custom-call | tf_op jit(solution)/shard_map/pallas_call | solution.py:316
  225.7 0.0 all-to-all-done
  225.7 0.0 all-gather.8.cloned.1.call-done.wm_ref
  225.7 1.1 copy-done
  226.8 45.8 %shard_map.154 = (bf16[1024,768]{1,0:T(8,128)(2,1)}, f32[1024,768]{1,0:T(8,128)}, bf16[1024,768]{1,0:T(8,128)(2,1)}, bf16[4,768,1536]{2,1,0:T(8,128)(2,1)}, f32[1,768]{1,0:T(1,128)}) custom-call(s32[1]{0:T(128)} %dynamic_slice.3.len_ref, bf16[1024,768]{1,0:T(8,128)(2,1)} %bitcast.55, f32[8,768]{1,0:T(8,128)} %pad.4.gains_ref, ...), custom_call_target="tpu_custom_call" | custom-call | tf_op jit(solution)/shard_map/pallas_call | solution.py:316
  272.6 49.4 %shard_map.155 = (bf16[1024,768]{1,0:T(8,128)(2,1)}, bf16[768,3072]{1,0:T(8,128)(2,1)}, f32[1,768]{1,0:T(1,128)}) custom-call(s32[1]{0:T(128)} %dynamic_slice.3.len_ref, bf16[1024,768]{1,0:T(8,128)(2,1)} %bitcast.50, f32[8,768]{1,0:T(8,128)} %pad.4.gains_ref, bf16[768,3072]{1,0:T(8,128)(2,1)} %all-gather.6.cloned.1.call-done.wa_ref, ...), custom_call_target="tpu_custom_call" | custom-call | tf_op jit(solution)/shard_map/pallas_call | solution.py:316
  322.0 7.3 %convert_element_type.16 = f32[768,3072]{1,0:T(8,128)} convert(bf16[768,3072]{1,0:T(8,128)(2,1)} %get-tuple-element.31) | non-fusion elementwise | flops 2359296 | bytes 14155776 | tf_op jit(solution)/shard_map/convert_element_type | solution.py:389
  329.3 0.0 reduce-scatter.6.cloned.1.call-update
  329.4 0.0 reduce-scatter.10.cloned.1.call-start
  329.4 16.1 %convert_element_type.17 = f32[4,768,1536]{2,1,0:T(8,128)} convert(bf16[4,768,1536]{2,1,0:T(8,128)(2,1)} %get-tuple-element.32) | non-fusion elementwise | flops 4718592 | bytes 28311552 | tf_op jit(solution)/shard_map/convert_element_type | solution.py:389
  345.5 0.0 reduce-scatter.10.cloned.1.call-update
  345.5 8.8 %reduce-scatter.8.cloned.1.call-start = ((), (), s32[]{:S(2)}) async-start(), calls=%async_computation.11 | async-start | bytes 1966080 | tf_op jit(solution)/shard_map/reduce_scatter | solution.py:394
  354.3 48.9 %reduce-scatter.6.cloned.1.call-done = f32[96,3072]{1,0:T(8,128)} async-done(((f32[768,3072]{1,0:T(8,128)}), f32[96,3072]{1,0:T(8,128)}) %reduce-scatter.6.cloned.1.call-update) | async-done | bytes 1179664 | tf_op jit(solution)/shard_map/reduce_scatter | solution.py:393
  403.3 2.9 copy.52
  406.2 0.0 reduce-scatter.8.cloned.1.call-update
  406.2 3.8 copy.60
  410.0 0.5 broadcast.2
  410.5 11.6 %reduce.1 = bf16[1024,768]{1,0:T(8,128)(2,1)} reduce(bf16[1024,1,768]{2,1,0:T(2,128)(2,1)S(1)} %bitcast.51, bf16[]{:T(256)} %broadcast.2), dimensions={1}, to_apply=%bitcast.47.reduce_sub_computation | reduce | bytes 3145730
  422.1 3.9 reshape.44
  426.1 4.5 all-to-all-start.3
  430.6 102.3 %reduce-scatter.10.cloned.1.call-done = f32[4,96,1536]{2,1,0:T(8,128)} async-done(((f32[4,768,1536]{2,1,0:T(8,128)}), f32[4,96,1536]{2,1,0:T(8,128)}) %reduce-scatter.10.cloned.1.call-update) | async-done | bytes 2359312 | tf_op jit(solution)/shard_map/reduce_scatter | solution.py:392
  532.9 0.0 reduce-scatter.12.cloned.1.call-update
  532.9 3.8 copy.61
  536.8 11.6 %reduce = bf16[1024,768]{1,0:T(8,128)(2,1)} reduce(bf16[1024,1,768]{2,1,0:T(2,128)(2,1)S(1)} %bitcast.52, bf16[]{:T(256)} %broadcast.2), dimensions={1}, to_apply=%bitcast.48.reduce_sub_computation | reduce | bytes 3145730
  548.4 3.7 reshape.46
  552.1 0.0 all-to-all-done.3
  552.1 4.7 all-to-all-start.2
  556.9 91.5 %all-reduce.1 = f32[2,768]{1,0:T(2,128)S(1)} all-reduce(f32[2,768]{1,0:T(2,128)S(1)} %pad_maximum_fusion.3), channel_id=7, replica_groups=mesh['dp'=8,'tp'=4] {'dp','tp'}, use_global_device_ids=true, to_apply=%region_4.5.clone | all-reduce | flops 1536 | bytes 12288
  648.4 0.6 constant_dynamic-slice_fusion
  649.1 3.0 reshape.45
  652.1 1.9 copy.54
  654.0 0.0 all-to-all-done.2
  654.0 3.1 reshape.47
  657.0 1.4 copy.53
  658.4 1.0 slice_bitcast_fusion
  659.4 0.9 copy.48
  660.3 1.5 slice_bitcast_fusion.4
  661.8 1.8 slice_bitcast_fusion.1
  663.7 0.8 pad_maximum_fusion
  (17 shorter events, 0.0 us)
Async XLA Ops:
  7.2 3.9 copy-start.2
  7.2 42.3 %all-gather.10.cloned.1.call-start = ((), (), s32[]{:S(2)}) async-start(), calls=%async_computation.14 | async-start | bytes 1474560 | tf_op jit(solution)/shard_map/all_gather | solution.py:381
  9.8 179.0 %all-gather.6.cloned.1.call-start = ((), (), s32[]{:S(2)}) async-start(), calls=%async_computation.8 | async-start | bytes 5308416 | tf_op jit(solution)/shard_map/all_gather | solution.py:380
  39.1 10.4 %copy-start.1 = (bf16[4,256,768]{2,1,0:T(8,128)(2,1)S(1)}, bf16[4,256,768]{2,1,0:T(8,128)(2,1)}, u32[]{:S(2)}) copy-start(bf16[4,256,768]{2,1,0:T(8,128)(2,1)} %param.10) | copy-start | bytes 4718596
  40.2 185.5 %all-gather.8.cloned.1.call-start = ((), (), s32[]{:S(2)}) async-start(), calls=%async_computation.9 | async-start | bytes 10616832 | tf_op jit(solution)/shard_map/all_gather | solution.py:381
  90.2 3.8 copy-start.5
  90.2 97.5 %copy-start.6 = (s32[4]{0:T(128)S(1)}, s32[4]{0:T(128)}, u32[]{:S(2)}) copy-start(s32[4]{0:T(128)} %param.11) | copy-start | bytes 52
  90.2 135.5 %all-to-all-start = ((bf16[4,256,768]{2,1,0:T(8,128)(2,1)}), bf16[4,256,768]{2,1,0:T(8,128)(2,1)S(1)}, u32[]{:S(2)}, u32[]{:S(2)}) async-start(bf16[4,256,768]{2,1,0:T(8,128)(2,1)} %param.17), calls=%async_computation | async-start | bytes 3145728 | tf_op jit(solution)/shard_map/all_to_all | solution.py:362
  93.9 309.4 %reduce-scatter.6.cloned.1.call-start = ((), (), s32[]{:S(2)}) async-start(), calls=%async_computation.10 | async-start | bytes 10616832 | tf_op jit(solution)/shard_map/reduce_scatter | solution.py:393
  225.7 1.1 copy-start
  329.4 203.5 %reduce-scatter.10.cloned.1.call-start = ((), (), s32[]{:S(2)}) async-start(), calls=%async_computation.12 | async-start | bytes 21233664 | tf_op jit(solution)/shard_map/reduce_scatter | solution.py:392
  345.5 312.9 %reduce-scatter.8.cloned.1.call-start = ((), (), s32[]{:S(2)}) async-start(), calls=%async_computation.11 | async-start | bytes 1966080 | tf_op jit(solution)/shard_map/reduce_scatter | solution.py:394
  426.1 126.1 %all-to-all-start.3 = ((bf16[4,2,98304]{2,1,0:T(2,128)(2,1)}), bf16[4,2,98304]{2,1,0:T(2,128)(2,1)}, u32[]{:S(2)}, u32[]{:S(2)}) async-start(bf16[4,2,98304]{2,1,0:T(2,128)(2,1)} %reshape.44), calls=%async_computation.3 | async-start | bytes 3145728 | tf_op jit(solution)/shard_map/all_to_all | solution.py:366
  430.6 231.2 %reduce-scatter.12.cloned.1.call-start = ((), (), s32[]{:S(2)}) async-start(), calls=%async_computation.13 | async-start | bytes 2949120 | tf_op jit(solution)/shard_map/reduce_scatter | solution.py:392
  552.1 4.8 copy-start.3
  552.1 4.8 copy-start.4
  552.1 101.9 %all-to-all-start.2 = ((bf16[4,2,98304]{2,1,0:T(2,128)(2,1)}), bf16[4,2,98304]{2,1,0:T(2,128)(2,1)}, u32[]{:S(2)}, u32[]{:S(2)}) async-start(bf16[4,2,98304]{2,1,0:T(2,128)(2,1)} %reshape.46), calls=%async_computation.2 | async-start | bytes 3145728 | tf_op jit(solution)/shard_map/all_to_all | solution.py:366
Sparse Core Ops, SparseCore 0:
  10.2 39.2 all-gather.9
  51.9 38.6 all-gather.5
  92.5 58.8 all-gather.7
  329.5 73.7 reduce-scatter.5
  406.7 126.1 reduce-scatter.9
  535.0 46.4 reduce-scatter.7
  583.8 55.5 reduce-scatter.11

commit v3 on v2

v3 whole, which is shorter than its diff:
```python
import functools

import numpy as np
import jax
import jax.numpy as jnp
from jax import lax
from jax.experimental import pallas as pl
from jax.experimental.pallas import tpu as pltpu
from jax.sharding import PartitionSpec as P

F32 = jnp.float32
BF16 = jnp.bfloat16
HEAD = 64
EPS = 1e-6
LOG2E = 1.4426950408889634
C2 = LOG2E * HEAD**-0.5
NEG = -1e30
BLK = 256


def dg(a, b, ca, cb):
    return lax.dot_general(a, b, (((ca,), (cb,)), ((), ())), preferred_element_type=F32)


def nn(a, b):
    return dg(a, b, 1, 0)


def nt(a, b):
    return dg(a, b, 1, 1)


def tn(a, b):
    return dg(a, b, 0, 0)


def rows_of(m):
    return pl.ds(pl.multiple_of(m * BLK, BLK), BLK)


def wa_cols(wa_ref, cols):
    part = wa_ref[:, :, :, cols]
    return part.reshape(-1, part.shape[-1])


def half_lane():
    return lax.broadcasted_iota(jnp.int32, (1, 128), 1) % HEAD < HEAD // 2


def head_lane(h):
    lane = lax.broadcasted_iota(jnp.int32, (1, 128), 1)
    return lane < HEAD if h == 0 else lane >= HEAD


def turned(v):
    return jnp.where(half_lane(), pltpu.roll(v, 96, 1), pltpu.roll(v, 32, 1))


def norm_rows(x, gain):
    r = lax.rsqrt(jnp.mean(x * x, axis=-1, keepdims=True) + EPS)
    return x * r, r


def norm_stage(t, x_ref, gains_ref, n1_ref):
    @pl.loop(0, t // BLK)
    def _(m):
        rs = rows_of(m)
        unit, _ = norm_rows(x_ref[rs, :].astype(F32), None)
        n1_ref[rs, :] = (unit * gains_ref[0:1, :]).astype(BF16)


def qkv_stage(t, d, n1_ref, wa_ref, cos_ref, sin_ref, q_ref, k_ref, v_ref):
    for c, out in enumerate((q_ref, k_ref, v_ref)):

        @pl.loop(0, d // 256)
        def _(j, c=c, out=out):
            cols = pl.ds(pl.multiple_of(c * d + j * 256, 256), 256)
            raw = nn(n1_ref[...], wa_cols(wa_ref, cols))
            for s in range(2):
                part = raw[:, s * 128 : (s + 1) * 128]
                if c < 2:
                    part = part * cos_ref[...] + turned(part) * sin_ref[...]
                out[:, pl.ds(pl.multiple_of(j * 256 + s * 128, 128), 128)] = part.astype(BF16)


def key_bias(t, length):
    pos = lax.broadcasted_iota(jnp.int32, (t, 1), 0)
    return jnp.where(pos < length, 0.0, NEG).astype(BF16)


def causal_block():
    key = lax.broadcasted_iota(jnp.int32, (BLK, BLK), 0)
    query = lax.broadcasted_iota(jnp.int32, (BLK, BLK), 1)
    return key <= query


def score_operands(h, qp, kp, bias):
    mine = head_lane(h)
    lane = lax.broadcasted_iota(jnp.int32, (1, 128), 1)
    spare = lane == (HEAD if h == 0 else 0)
    zero = jnp.zeros((), BF16)
    q_m = jnp.where(mine, qp, zero)
    k_m = jnp.where(mine, kp, zero)
    q_s = jnp.where(spare, jnp.ones((), BF16), q_m)
    k_s = jnp.where(spare, bias, k_m)
    return q_m, k_m, q_s, k_s


def mask_diag(s, i):
    if i == 0:
        return jnp.where(causal_block(), s, NEG)
    return jnp.concatenate([s[: i * BLK], jnp.where(causal_block(), s[i * BLK :], NEG)], axis=0)


def attend_stage(t, d, length, q_ref, k_ref, v_ref, ctxt_ref, lse_ref, first, last):
    bias = key_bias(t, length)

    @pl.loop(first, last)
    def _(p):
        cols = pl.ds(pl.multiple_of(p * 128, 128), 128)
        qp, kp, vp = q_ref[:, cols], k_ref[:, cols], v_ref[:, cols]
        for h in range(2):
            _, _, q_s, k_s = score_operands(h, qp, kp, bias)
            for i in range(t // BLK):
                n = (i + 1) * BLK
                s = mask_diag(nt(k_s[:n], q_s[i * BLK : n]), i)
                top = jnp.max(s, axis=0, keepdims=True)
                e = jnp.exp2((s - top) * C2)
                total = jnp.sum(e, axis=0, keepdims=True)
                o = tn(vp[:n], e.astype(BF16))[h * HEAD : (h + 1) * HEAD] / total
                ctxt_ref[pl.ds(pl.multiple_of(p * 128 + h * HEAD, HEAD), HEAD), i * BLK : n] = o.astype(BF16)
                lse_ref[pl.ds(p * 2 + h, 1), i * BLK : n] = top * C2 + jnp.log2(total)


def out_stage(t, d, length, x_ref, wa_ref, ctxt_ref, hid_ref):
    out = dg(ctxt_ref[...], wa_cols(wa_ref, slice(3 * d, 4 * d)), 0, 1)
    pos = lax.broadcasted_iota(jnp.int32, (t, 1), 0)
    hid_ref[...] = x_ref[...].astype(F32) + jnp.where(pos < length, out, 0.0)


def k1_alone(len_ref, x_ref, gains_ref, wa_ref, cos_ref, sin_ref, q_ref, k_ref, v_ref, ctxt_ref, lse_ref, hid_ref, n1_ref):
    t, d = x_ref.shape
    length = len_ref[0]
    norm_stage(t, x_ref, gains_ref, n1_ref)
    qkv_stage(t, d, n1_ref, wa_ref, cos_ref, sin_ref, q_ref, k_ref, v_ref)
    attend_stage(t, d, length, q_ref, k_ref, v_ref, ctxt_ref, lse_ref, 0, d // 128)
    out_stage(t, d, length, x_ref, wa_ref, ctxt_ref, hid_ref)


def token_mask(m, length):
    pos = m * BLK + lax.broadcasted_iota(jnp.int32, (BLK, 1), 0)
    return pos < length


def mlp_chunk(t, d, f, wm, gm, n2_ref, dm_ref, n2t_ref, dmt_ref, act_ref, dgu_ref, mlp_ref, dn2_ref):
    w = 256

    def wcols(lo, hi):
        return wm[:, :, :, lo:hi].reshape(d, hi - lo)

    def put(lo, hi, value):
        gm[:, :, :, lo:hi] = value.astype(BF16).reshape(gm.shape[:3] + (hi - lo,))

    for j in range(f // w):
        lo, hi = j * w, (j + 1) * w
        gate = nn(n2_ref[...], wcols(lo, hi))
        up = nn(n2_ref[...], wcols(f + lo, f + hi))
        d_act = nn(dm_ref[...], wcols(2 * f + lo, 2 * f + hi))
        s = 1.0 / (1.0 + jnp.exp2(gate * (-LOG2E)))
        sw = gate * s
        act_ref[:, lo:hi] = (sw * up).astype(BF16)
        dgu_ref[:, lo:hi] = (d_act * up * (s + sw * (1.0 - s))).astype(BF16)
        dgu_ref[:, f + lo : f + hi] = (d_act * sw).astype(BF16)

    mlp_ref[...] += nt(act_ref[...], wcols(2 * f, 3 * f))
    dn2_ref[...] += nt(dgu_ref[...], wcols(0, 2 * f))
    for j in range(2 * f // w):
        put(j * w, (j + 1) * w, nn(n2t_ref[...], dgu_ref[:, j * w : (j + 1) * w]))
    for j in range(f // w):
        put(2 * f + j * w, 2 * f + (j + 1) * w, nn(dmt_ref[...], act_ref[:, j * w : (j + 1) * w]))


def k2(len_ref, cot_ref, gains_ref, hid_ref, wm_ref, lo_ref, dh_ref, da_ref, gm_ref, gg_ref,
       n2_ref, dm_ref, n2t_ref, dmt_ref, act_ref, dgu_ref, mlp_ref, dn2_ref):
    t, d = cot_ref.shape
    tp, f = wm_ref.shape[0], wm_ref.shape[-1] // 3
    length = len_ref[0]

    @pl.loop(0, t // BLK)
    def _(m):
        rs = rows_of(m)
        unit, _ = norm_rows(hid_ref[rs, :], None)
        n2 = (unit * gains_ref[1:2, :]).astype(BF16)
        n2_ref[rs, :] = n2
        n2t_ref[:, rs] = n2.T
        dm = jnp.where(token_mask(m, length), cot_ref[rs, :], jnp.zeros((), BF16))
        dm_ref[rs, :] = dm
        dmt_ref[:, rs] = dm.T

    mlp_ref[...] = jnp.zeros_like(mlp_ref)
    dn2_ref[...] = jnp.zeros_like(dn2_ref)

    @pl.loop(0, tp)
    def _(z):
        mlp_chunk(t, d, f, wm_ref.at[z], gm_ref.at[z], n2_ref, dm_ref, n2t_ref, dmt_ref, act_ref, dgu_ref, mlp_ref, dn2_ref)

    gg_ref[...] = jnp.zeros_like(gg_ref)

    @pl.loop(0, t // BLK)
    def _(m):
        rs = rows_of(m)
        hid = hid_ref[rs, :]
        ok = token_mask(m, length)
        lo_ref[rs, :] = (hid + jnp.where(ok, mlp_ref[rs, :], 0.0)).astype(BF16)
        unit, r = norm_rows(hid, None)
        dn2 = dn2_ref[rs, :]
        gg_ref[...] += jnp.sum(dn2 * unit, axis=0, keepdims=True)
        e2 = dn2 * gains_ref[1:2, :]
        dh = cot_ref[rs, :].astype(F32) + r * (e2 - unit * jnp.mean(e2 * unit, axis=-1, keepdims=True))
        dh_ref[rs, :] = dh
        da_ref[rs, :] = jnp.where(ok, dh, 0.0).astype(BF16)


def k3(len_ref, x_ref, gains_ref, wa_ref, cos_ref, sin_ref, q_ref, k_ref, v_ref, ctxt_ref, lse_ref, dh_ref, da_ref,
       gx_ref, ga_ref, gg_ref, n1_ref, n1t_ref, dat_ref, dctx_ref, dlt_ref, dqkv_ref, dk_acc, dv_acc, dn1_ref):
    t, d = x_ref.shape
    length = len_ref[0]

    dat_ref[...] = da_ref[...].T

    @pl.loop(0, d // 256)
    def _(j):
        rs = pl.ds(pl.multiple_of(j * 256, 256), 256)
        cols = pl.ds(pl.multiple_of(3 * d + j * 256, 256), 256)
        ga_ref[:, :, :, cols] = nt(dat_ref[...], ctxt_ref[rs, :]).astype(BF16).reshape(ga_ref.shape[:3] + (256,))
        dctx = nn(da_ref[...], wa_cols(wa_ref, cols)).astype(BF16)
        dctx_ref[:, rs] = dctx
        prod = dctx.T.astype(F32) * ctxt_ref[rs, :].astype(F32)
        for h in range(4):
            dlt_ref[pl.ds(j * 4 + h, 1), :] = jnp.sum(prod[h * HEAD : (h + 1) * HEAD], axis=0, keepdims=True)

    bias = key_bias(t, length)

    @pl.loop(0, d // 128)
    def _(p):
        cols = pl.ds(pl.multiple_of(p * 128, 128), 128)
        qp, kp, vp, gp = q_ref[:, cols], k_ref[:, cols], v_ref[:, cols], dctx_ref[:, cols]
        dk_acc[...] = jnp.zeros_like(dk_acc)
        dv_acc[...] = jnp.zeros_like(dv_acc)
        ops = [score_operands(h, qp, kp, bias) for h in range(2)]
        for i in range(t // BLK):
            n = (i + 1) * BLK
            qs = slice(i * BLK, n)
            dq = None
            for h in range(2):
                q_m, k_m, q_s, k_s = ops[h]
                g_m = jnp.where(head_lane(h), gp[qs], jnp.zeros((), BF16))
                s = mask_diag(nt(k_s[:n], q_s[qs]), i)
                pr = jnp.exp2(s * C2 - lse_ref[pl.ds(p * 2 + h, 1), qs])
                dp = nt(vp[:n], g_m)
                ds = (pr * (dp - dlt_ref[pl.ds(p * 2 + h, 1), qs])).astype(BF16)
                dv_acc[:n, :] += nn(pr.astype(BF16), g_m)
                dk_acc[:n, :] += nn(ds, q_m[qs])
                part = tn(ds, k_m[:n])
                dq = part if dq is None else dq + part
            dq = dq * (HEAD**-0.5)
            dqkv_ref[qs, cols] = (dq * cos_ref[qs, :] - turned(dq) * sin_ref[qs, :]).astype(BF16)
        dk = dk_acc[...] * (HEAD**-0.5)
        dqkv_ref[:, pl.ds(pl.multiple_of(d + p * 128, 128), 128)] = (dk * cos_ref[...] - turned(dk) * sin_ref[...]).astype(BF16)
        dqkv_ref[:, pl.ds(pl.multiple_of(2 * d + p * 128, 128), 128)] = dv_acc[...].astype(BF16)

    @pl.loop(0, t // BLK)
    def _(m):
        rs = rows_of(m)
        unit, _ = norm_rows(x_ref[rs, :].astype(F32), None)
        n1t_ref[:, rs] = (unit * gains_ref[0:1, :]).astype(BF16).T

    @pl.loop(0, 3 * d // 256)
    def _(j):
        cols = pl.ds(pl.multiple_of(j * 256, 256), 256)
        ga_ref[:, :, :, cols] = nn(n1t_ref[...], dqkv_ref[:, cols]).astype(BF16).reshape(ga_ref.shape[:3] + (256,))

    dn1_ref[...] = nt(dqkv_ref[...], wa_cols(wa_ref, slice(0, 3 * d)))

    gg_ref[...] = jnp.zeros_like(gg_ref)

    @pl.loop(0, t // BLK)
    def _(m):
        rs = rows_of(m)
        unit, r = norm_rows(x_ref[rs, :].astype(F32), None)
        dn1 = dn1_ref[rs, :]
        gg_ref[...] += jnp.sum(dn1 * unit, axis=0, keepdims=True)
        e1 = dn1 * gains_ref[0:1, :]
        gx_ref[rs, :] = (dh_ref[rs, :] + r * (e1 - unit * jnp.mean(e1 * unit, axis=-1, keepdims=True))).astype(BF16)


def rope_np(t):
    half = HEAD // 2
    freqs = np.float32(10000.0) ** (np.float32(-2.0) * np.arange(half, dtype=np.float32) / np.float32(HEAD))
    ang = np.arange(t, dtype=np.float32)[:, None] * freqs[None, :].astype(np.float32)
    c, s = np.cos(ang), np.sin(ang)
    return np.concatenate([c, c, c, c], 1).astype(np.float32), np.concatenate([-s, s, -s, s], 1).astype(np.float32)


MESH = pl.DeviceIdType.MESH
Z = 4


def flip(d, bit):
    return d + bit - 2 * bit * lax.rem(d // bit, 2)


class Net:
    def __init__(self, send, recv, local):
        self.d, self.z = lax.axis_index("dp"), lax.axis_index("tp")
        self.yx, self.c = self.d // 2, lax.rem(self.d, 2)
        self.x, self.y, self.core = ((flip(self.d, b), self.z) for b in (2, 4, 1))
        self.send, self.recv, self.local = send, recv, local
        self.copies, self.own = {}, {}

    def peer(self, r):
        return lax.rem(self.z + r, Z)

    def source(self, r):
        return lax.rem(self.z + Z - r, Z)

    def barrier(self):
        sem = pltpu.get_barrier_semaphore()
        for dev in (self.x, self.y, self.core) + tuple((self.d, self.peer(r)) for r in range(1, Z)):
            pl.semaphore_signal(sem, inc=1, device_id=dev, device_id_type=MESH)
        pl.semaphore_wait(sem, 6)

    def start(self, name, src, dst, dev):
        i = len(self.copies)
        copy = pltpu.make_async_remote_copy(
            src_ref=src, dst_ref=dst, send_sem=self.send.at[i], recv_sem=self.recv.at[i], device_id=dev, device_id_type=MESH
        )
        copy.start()
        self.copies[name] = copy

    def keep(self, name, src, dst):
        copy = pltpu.make_async_copy(src, dst, self.local.at[len(self.own)])
        copy.start()
        self.own[name] = copy

    def got(self, *names):
        for name in names:
            self.copies[name].wait_recv()

    def kept(self, name):
        self.own[name].wait()

    def finish(self):
        for copy in self.copies.values():
            copy.wait_send()


def spread(net, tag, own, slab, halves):
    net.start(tag + "x", own, slab(net.yx), net.x)
    net.start(tag + "y", own, slab(net.yx), net.y)


def relay(net, tag, slab, halves):
    kx, ky = flip(net.yx, 1), flip(net.yx, 2)
    net.got(tag + "x")
    net.start(tag + "l", slab(kx).at[:, halves[0]], slab(kx).at[:, halves[0]], net.y)
    net.got(tag + "y")
    net.start(tag + "r", slab(ky).at[:, halves[1]], slab(ky).at[:, halves[1]], net.x)


def all_sum(net, tag, own, boxes):
    for r in range(1, Z):
        net.start(f"{tag}z{r}", own, boxes.at[r - 1], (net.d, net.peer(r)))
    yield
    net.got(*(f"{tag}z{r}" for r in range(1, Z)))
    boxes[6] = own[...] + (boxes[0] + boxes[1] + boxes[2])
    net.start(tag + "x", boxes.at[6], boxes.at[3], net.x)
    yield
    net.got(tag + "x")
    boxes[7] = boxes[6] + boxes[3]
    net.start(tag + "y", boxes.at[7], boxes.at[4], net.y)
    yield
    net.got(tag + "y")
    boxes[8] = boxes[7] + boxes[4]
    net.start(tag + "c", boxes.at[8], boxes.at[5], net.core)
    yield
    net.got(tag + "c")
    boxes[9] = boxes[8] + boxes[5]
    yield


def lane_pairs(stage, hw):
    low = lax.broadcasted_iota(jnp.int32, (1, 128), 1) < HEAD
    parts = [[stage[z][:, c * 128 : (c + 1) * 128] for z in range(Z)] for c in range(4)]
    for j in range(Z // 2):
        for g in range(2):
            cols = slice(512 + g * 128, 640 + g * 128)
            a, b = stage[2 * j][:, cols].astype(F32), stage[2 * j + 1][:, cols].astype(F32)
            parts[2 * g].append(jnp.where(low, a, pltpu.roll(b, HEAD, 1)).astype(BF16))
            parts[2 * g + 1].append(jnp.where(low, pltpu.roll(a, HEAD, 1), b).astype(BF16))
    return parts


def k1(len_ref, tok_ref, cot_ref, was_ref, wms_ref, gs_ref, cos_ref, sin_ref,
       x_ref, cotw_ref, wa_ref, wm_ref, gains_ref, q_ref, k_ref, v_ref, ctxt_ref, lse_ref, hid_ref,
       n1_ref, stage_ref, boxes_ref, send, recv, local):
    t, d = x_ref.shape
    part = t // Z
    rows = wms_ref.shape[0]
    length = len_ref[0]
    net = Net(send, recv, local)
    z, yx, c = net.z, net.yx, net.c
    mine = pl.ds(pl.multiple_of(z * part, part), part)
    a_half = (slice(0, 2 * d), slice(2 * d, 4 * d))
    f3 = wms_ref.shape[1]
    m_half = (slice(0, f3 // 2), slice(f3 // 2, f3))
    a_slab = lambda k: wa_ref.at[k, c]
    m_slab = lambda w: lambda k: wm_ref.at[w, k, c]

    net.barrier()
    gains_steps = all_sum(net, "g", gs_ref, boxes_ref)
    next(gains_steps)
    for r in range(1, Z):
        net.start(f"az{r}", was_ref, stage_ref.at[z], (net.d, net.peer(r)))
    net.keep("a", was_ref, stage_ref.at[z])
    net.keep("m", wms_ref, wm_ref.at[z, yx, c])
    spread(net, "m0", wms_ref, m_slab(z), m_half)
    for r in range(1, Z):
        net.start(f"t{r}", tok_ref.at[net.peer(r)], x_ref.at[mine], (net.d, net.peer(r)))
    net.keep("t", tok_ref.at[z], x_ref.at[mine])
    next(gains_steps)

    net.got(*(f"az{r}" for r in range(1, Z)))
    net.kept("a")
    for i, heads in enumerate(lane_pairs(stage_ref, 4 * d // Z)):
        for j, value in enumerate(heads):
            wa_ref[yx, c, :, i * d + j * 128 : i * d + (j + 1) * 128] = value
    spread(net, "a", wa_ref.at[yx, c], a_slab, a_half)
    net.start("ac0", wa_ref.at[yx, c], wa_ref.at[yx, c], net.core)
    next(gains_steps)
    next(gains_steps)
    relay(net, "m0", m_slab(z), m_half)
    next(gains_steps)
    gains_ref[...] = boxes_ref[9]
    net.got(*(f"t{r}" for r in range(1, Z)))
    net.kept("t")
    for r in range(1, Z):
        net.start(f"mz{r}", wms_ref, wm_ref.at[z, yx, c], (net.d, net.peer(r)))
    norm_stage(t, x_ref, gains_ref, n1_ref)
    relay(net, "a", a_slab, a_half)
    net.start("ac1", wa_ref.at[flip(yx, 1), c], wa_ref.at[flip(yx, 1), c], net.core)
    net.start("ac2", wa_ref.at[flip(yx, 2), c], wa_ref.at[flip(yx, 2), c], net.core)
    net.got("al", "ar")
    kd = flip(flip(yx, 1), 2)
    net.start("ac3", wa_ref.at[kd, c], wa_ref.at[kd, c], net.core)
    net.got("m0l", "m0r")
    net.kept("m")
    net.start("m0c", wm_ref.at[z, :, c], wm_ref.at[z, :, c], net.core)
    net.got("ac0", "ac1", "ac2", "ac3")
    qkv_stage(t, d, n1_ref, wa_ref, cos_ref, sin_ref, q_ref, k_ref, v_ref)
    attend = functools.partial(attend_stage, t, d, length, q_ref, k_ref, v_ref, ctxt_ref, lse_ref)
    attend(0, 3)
    for r in range(1, Z):
        w = net.source(r)
        net.got(f"mz{r}")
        spread(net, f"m{r}", wm_ref.at[w, yx, c], m_slab(w), m_half)
    for r in range(1, Z):
        net.start(f"c{r}", cot_ref.at[net.peer(r)], cotw_ref.at[mine], (net.d, net.peer(r)))
    net.keep("c", cot_ref.at[z], cotw_ref.at[mine])
    attend(3, d // 128)
    out_stage(t, d, length, x_ref, wa_ref, ctxt_ref, hid_ref)
    for r in range(1, Z):
        relay(net, f"m{r}", m_slab(net.source(r)), m_half)
    for r in range(1, Z):
        w = net.source(r)
        net.got(f"m{r}l", f"m{r}r")
        net.start(f"m{r}c", wm_ref.at[w, :, c], wm_ref.at[w, :, c], net.core)
    net.got(*(f"m{r}c" for r in range(Z)), *(f"c{r}" for r in range(1, Z)))
    net.kept("c")
    net.finish()


VM = pl.BlockSpec(memory_space=pltpu.VMEM)
SM = pl.BlockSpec(memory_space=pltpu.SMEM)


def call(kernel, ins, outs, scratch):
    return pl.pallas_call(
        kernel,
        out_shape=[jax.ShapeDtypeStruct(s, dt) for s, dt in outs],
        in_specs=[SM] + [VM] * (len(ins) - 1),
        out_specs=[VM] * len(outs),
        scratch_shapes=[pltpu.VMEM(s, dt) for s, dt in scratch],
        compiler_params=pltpu.CompilerParams(vmem_limit_bytes=60 * 2**20),
    )(*ins)


def backward(length, x, cot, gains, wa, wm, cosine, sine, q, k, v, ctxt, lse, hid):
    t, d = x.shape
    f = wm.shape[-1] // 3
    heads = lse.shape[0]
    td, dt = ((t, d), BF16), ((d, t), BF16)
    lo, dh, da, gm, gg2 = call(
        k2,
        (length, cot, gains, hid, wm),
        (td, ((t, d), F32), td, (wm.shape, BF16), ((1, d), F32)),
        (td, td, dt, dt, ((t, f), BF16), ((t, 2 * f), BF16), ((t, d), F32), ((t, d), F32)),
    )
    gx, ga, gg1 = call(
        k3,
        (length, x, gains, wa, cosine, sine, q, k, v, ctxt, lse, dh, da),
        (td, (wa.shape, BF16), ((1, d), F32)),
        (td, dt, dt, td, ((heads, t), F32), ((t, 3 * d), BF16), ((t, 128), F32), ((t, 128), F32), ((t, d), F32)),
    )
    return lo, gx, ga, gm, jnp.concatenate([gg1, gg2])


def one_sequence(length, x, cot, gains, wa, wm, cosine, sine):
    t, d = x.shape
    heads = -(-d // HEAD // 8) * 8
    td, dt = ((t, d), BF16), ((d, t), BF16)
    kept = call(k1_alone, (length, x, gains, wa, cosine, sine), (td, td, td, dt, ((heads, t), F32), ((t, d), F32)), (td,))
    return backward(length, x, cot, gains, wa, wm, cosine, sine, *kept)


def pack_weights(w_qkv, w_out, w_gate_up, w_down):
    attn = jnp.stack([w_qkv[0], w_qkv[1], w_qkv[2], w_out.T], axis=1)
    mlp = jnp.concatenate([w_gate_up[0], w_gate_up[1], w_down.T], axis=1)
    return attn, mlp


def unpack_grads(g_attn, g_mlp, fw):
    g_qkv = jnp.transpose(g_attn[:, :3], (1, 0, 2))
    g_gate_up = jnp.stack([g_mlp[:, i * fw : (i + 1) * fw] for i in range(2)])
    return g_qkv, g_attn[:, 3].T, g_gate_up, g_mlp[:, 2 * fw :].T


def to_sequences(local):
    return lax.all_to_all(local, "tp", split_axis=0, concat_axis=1, tiled=True)


def to_positions(whole):
    return lax.all_to_all(whole, "tp", split_axis=1, concat_axis=0, tiled=True)


def fused_forward(length, tokens, cotangent, attn, mlp, gains, cosine, sine):
    batch, part, d = tokens.shape
    t, rows, hw = part * Z, attn.shape[0], attn.shape[2]
    heads = -(-d // HEAD // 8) * 8
    pairs = 2 * HEAD
    was = jnp.concatenate(
        [attn[:, :, :pairs].reshape(rows, 4 * pairs), attn[:, :, pairs:].reshape(rows, 4 * HEAD)], axis=1
    )
    spot = (lax.axis_index("dp") * Z + lax.axis_index("tp")) * gains.shape[1]
    gs = lax.dynamic_update_slice(jnp.zeros((8, d), F32), gains, (0, spot))
    f3 = mlp.shape[1]
    td, dt = ((t, d), BF16), ((d, t), BF16)
    outs = (
        td, td, ((4, 2, rows, 4 * d), BF16), ((Z, 4, 2, rows, f3), BF16), ((8, d), F32),
        td, td, td, dt, ((heads, t), F32), ((t, d), F32),
    )
    hbm = pl.BlockSpec(memory_space=pl.ANY)
    out_specs = [VM, hbm, VM, hbm] + [VM] * 7
    return pl.pallas_call(
        k1,
        out_shape=[jax.ShapeDtypeStruct(s, dt_) for s, dt_ in outs],
        in_specs=[SM, hbm, hbm, VM, hbm, VM, VM, VM],
        out_specs=out_specs,
        scratch_shapes=[
            pltpu.VMEM((t, d), BF16),
            pltpu.VMEM((Z, rows, d), BF16),
            pltpu.VMEM((10, 8, d), F32),
            pltpu.SemaphoreType.DMA((64,)),
            pltpu.SemaphoreType.DMA((64,)),
            pltpu.SemaphoreType.DMA((8,)),
        ],
        compiler_params=pltpu.CompilerParams(collective_id=0, has_side_effects=True, vmem_limit_bytes=60 * 2**20),
    )(length, tokens, cotangent, was, mlp, gs, cosine, sine)


def fits(mesh_dp, tokens, w_qkv, w_gate_up):
    tp = lax.axis_size("tp")
    rows, hw = w_qkv.shape[1:]
    return (
        mesh_dp == 8 and tp == Z and tokens.shape[0] == Z and hw == 3 * HEAD and rows % 16 == 0
        and w_gate_up.shape[2] % 256 == 0 and tokens.shape[1] % BLK == 0
    )


def body(tokens, lengths, w_qkv, w_out, w_gate_up, w_down, gains, cotangent):
    tp, dp = lax.axis_size("tp"), lax.axis_size("dp")
    batch, part, d = tokens.shape
    n, t = batch // tp, part * tp
    fw = w_gate_up.shape[2]
    cosine, sine = map(jnp.asarray, rope_np(t))
    attn, mlp = pack_weights(w_qkv, w_out, w_gate_up, w_down)
    own = lax.dynamic_slice_in_dim(lengths, lax.axis_index("tp") * n, n)
    if fits(dp, tokens, w_qkv, w_gate_up):
        x, cot, wa, wm, full_gains, *kept = fused_forward(own, tokens, cotangent, attn, mlp, gains, cosine, sine)
        lo, gx, ga, gm, gg = backward(own, x, cot, full_gains, wa, wm, cosine, sine, *kept)
        out, gx = to_positions(lo[None]), to_positions(gx[None]).astype(F32)
        ga, gm = ga.astype(F32).reshape(d, 4, d), gm.astype(F32).reshape(tp, d, 3 * fw)
        pairs = ga[:, :, : 2 * HEAD * Z].reshape(d, 4, Z, 2 * HEAD)
        third = ga[:, :, 2 * HEAD * Z :].reshape(d, 4, Z, HEAD)
        ga = jnp.concatenate([pairs, third], axis=3).reshape(d, 4, d)
    else:
        full_gains = lax.all_gather(gains, ("dp", "tp"), axis=1, tiled=True)
        full_gains = jnp.pad(full_gains, ((0, 6), (0, 0)))
        x16 = to_sequences(tokens)
        wa = lax.all_gather(attn, "tp", axis=2, tiled=True).reshape(attn.shape[0], 4 * d)
        wa = lax.all_gather(wa, "dp", axis=0, tiled=True).reshape(1, 1, d, 4 * d)
        wm = lax.all_gather(lax.all_gather(mlp, "tp", axis=0), "dp", axis=1, tiled=True).reshape(tp, 1, 1, d, 3 * fw)
        cot16 = to_sequences(cotangent)
        los, gxs, ga, gm, gg = [], [], 0.0, 0.0, 0.0
        for i in range(n):
            lo, gx, a, m, g = one_sequence(own[i : i + 1], x16[i], cot16[i], full_gains, wa, wm, cosine, sine)
            los.append(lo)
            gxs.append(gx)
            ga, gm, gg = ga + a.astype(F32), gm + m.astype(F32), gg + g
        out = to_positions(jnp.stack(los))
        gx = to_positions(jnp.stack(gxs)).astype(F32)
        ga, gm = ga.reshape(d, 4, d), gm.reshape(tp, d, 3 * fw)
    s_mlp = lax.psum_scatter(lax.psum_scatter(gm, "dp", scatter_dimension=1, tiled=True), "tp", scatter_dimension=0)
    s_attn = lax.psum_scatter(ga.reshape(d, 4 * d), "dp", scatter_dimension=0, tiled=True)
    s_attn = lax.psum_scatter(s_attn.reshape(-1, 4, d), "tp", scatter_dimension=2, tiled=True)
    s_gains = lax.psum_scatter(gg, ("dp", "tp"), scatter_dimension=1, tiled=True)
    return (out, gx) + unpack_grads(s_attn, s_mlp, fw) + (s_gains,)


def solution(mesh):
    act = P("dp", "tp", None)
    cols, rows, gain = P(None, "dp", "tp"), P("tp", "dp"), P(None, ("dp", "tp"))
    return jax.shard_map(
        body,
        mesh=mesh,
        in_specs=(act, P("dp"), cols, rows, cols, rows, gain, act),
        out_specs=(act, act, cols, rows, cols, rows, gain),
        check_vma=False,
    )
```

time: 679 us -> 646 us (0.951)
  blocking collectives: 254 us -> 92 us
  Pallas kernels: 132 us -> 214 us
  local copies, waits for them, and re-layouts: 39.6 us -> 76 us
  waiting for transfers between devices: 161 us -> 182 us
  starting transfers between devices: 22 us -> 9.48 us
    all_gather x2 -> x0, blocking collectives: 122 us -> none  [the longest x1 93.6 us: body(): full_gains = lax.all_gather(gains, ('dp', 'tp'), axis=1, tiled=True)]
    pallas_call x0 -> x1, Pallas kernels: none -> 118 us  [fused_forward(): pl.pallas_call(k1, out_shape=[jax.ShapeDtypeStruct(s, dt_) for s, dt_ in...]
    unnamed x7 -> x5, waiting for transfers between devices: 0.11 us -> 79.8 us
    reduce_scatter x1 -> x0, waiting for transfers between devices: 48.9 us -> none  [body(): s_attn = lax.psum_scatter(ga, 'dp', scatter_dimension=0, tiled=True)]
    all_to_all x1 -> x0, blocking collectives: 40.6 us -> none  [to_sequences(): return lax.all_to_all(local, 'tp', split_axis=0, concat_axis=1, tiled=True)]
    pallas_call x3 -> x2, Pallas kernels: 132 us -> 95.3 us  [call(): pl.pallas_call(kernel, out_shape=[jax.ShapeDtypeStruct(s, dt) for s, dt i...]
    convert_element_type x2 -> x0, other arithmetic: 23.4 us -> none  [body(): ga, gm, gg = (ga + a.astype(F32), gm + m.astype(F32), gg + g)]
    unnamed x27 -> x25, local copies, waits for them, and re-layouts: 20.6 us -> 35.3 us
  transfers between devices with their start and end apart: 10 -> 6, of which waited for: 3 -> 2; matrix products, arithmetic and copies ran while one was open for 11% -> 11% of each run, Pallas kernels for 5% -> 0%
where the time goes in v3:
time: 646 us; the launch traced here: 636 us
  Pallas kernels  214 us (33%)
  waiting for transfers between devices  182 us (28%)
  blocking collectives  92 us (14%)
  local copies, waits for them, and re-layouts  76 us (12%)
  other arithmetic  48.1 us (7%)
  between operations  14.3 us (2%)
  starting transfers between devices  9.48 us (1%)
    pallas_call x1, Pallas kernels, fused_forward(): pl.pallas_call(k1, out_shape=[jax.ShapeDtypeStruct(s, dt_) for s, dt_ in...  118 us
    reduce_scatter x1, waiting for transfers between devices, body(): lax.psum_scatter(gm, 'dp', scatter_dimension=1, tiled=True)  102 us
    pallas_call x2, Pallas kernels, call(): pl.pallas_call(kernel, out_shape=[jax.ShapeDtypeStruct(s, dt) for s, dt i...  95.3 us
    unnamed x1, blocking collectives  92 us
    unnamed x5, waiting for transfers between devices  79.8 us
    unnamed x25, local copies, waits for them, and re-layouts  35.3 us
    unnamed x2, other arithmetic  23.2 us
  transfers between devices with their start and end apart: 6, of which 2 were waited for; matrix products, arithmetic and copies ran while one was open for 11% of the time, Pallas kernels for 0%

profile of v3, /device:TPU:0, one launch (start us, length us, event | category | flops | bytes accessed | tf_op | source)
XLA Modules:
  0.0 635.7 jit_solution(17092310734882155817)
XLA Ops:
  7.2 0.0 copy-start.4
  7.2 0.0 reduce-scatter.14.cloned.1.call-start
  7.2 0.9 fusion
  8.1 0.1 copy.63
  8.2 0.1 copy.62
  8.3 0.1 copy.61
  8.4 0.7 pad_maximum_fusion.5
  9.2 0.9 pad_maximum_fusion.3
  10.0 0.1 copy.47
  10.2 0.1 copy.57
  10.3 1.0 slice_bitcast_fusion.6
  11.2 1.2 dynamic_slice.3.len_ref
  12.5 0.7 pad_maximum_fusion.4.was_ref
  13.2 1.6 pad_maximum_fusion.2.wms_ref
  14.8 0.0 copy-done.4
  14.8 0.3 dynamic_update_slice.3.gs_ref
  15.1 0.0 copy-start.1
  15.1 0.6 copy-done.1
  15.7 118.3 %shard_map.153 = (bf16[1024,768]{1,0:T(8,128)(2,1)}, bf16[1024,768]{1,0:T(8,128)(2,1)}, bf16[4,2,96,3072]{3,2,1,0:T(8,128)(2,1)}, bf16[4,4,2,96,1536]{4,3,2,1,0:...) custom-call(s32[1]{0:T(128)} %dynamic_slice.3.len_ref, ...), custom_call_target="tpu_custom_call" | custom-call | tf_op jit(solution)/shard_map/pallas_call | solution.py:564
  134.0 45.9 %shard_map.154 = (bf16[1024,768]{1,0:T(8,128)(2,1)}, f32[1024,768]{1,0:T(8,128)}, bf16[1024,768]{1,0:T(8,128)(2,1)}, bf16[4,4,2,96,1536]{4,3,2,1,0:T(8,128)(2,1)}, f32[1,768]{1,0:T(1,128)}) custom-call(s32[1]{0:T(128)} %dynamic_slice.3.len_ref, bf16[1024,768]{1,0:T(8,128)(2,1)} %get-tuple-element.26.cot_ref, f32[8,768]{1,0:T(8,128)} %get-tuple-element.27.gains_ref, ...), custom_call_target="tpu_custom_call" | custom-call | tf_op jit(solution)/shard_map/pallas_call | solution.py:488
  179.9 49.4 %shard_map.155 = (bf16[1024,768]{1,0:T(8,128)(2,1)}, bf16[4,2,96,3072]{3,2,1,0:T(8,128)(2,1)}, f32[1,768]{1,0:T(1,128)}) custom-call(s32[1]{0:T(128)} %dynamic_slice.3.len_ref, bf16[1024,768]{1,0:T(8,128)(2,1)} %get-tuple-element.31.x_ref, f32[8,768]{1,0:T(8,128)} %get-tuple-element.27.gains_ref, bf16[4,2,96,3072]{3,2,1,0:T(8,128)(2,1)} %get-tuple-element.32.wa_ref, ...), custom_call_target="tpu_custom_call" | custom-call | tf_op jit(solution)/shard_map/pallas_call | solution.py:488
  229.3 10.6 %reshape.60 = f32[768,4,768]{2,1,0:T(4,128)} reshape(bf16[4,2,96,3072]{3,2,1,0:T(8,128)(2,1)} %get-tuple-element.41) | data formatting | bytes 14155776 | tf_op jit(solution)/shard_map/reshape | solution.py:602
  239.9 6.7 %slice.57 = f32[768,4,512]{2,1,0:T(4,128)} slice(f32[768,4,768]{2,1,0:T(4,128)} %reshape.60), slice={[0:768], [0:4], [0:512]} | slice | bytes 12582912 | tf_op jit(solution)/shard_map/slice | solution.py:603
  246.6 0.0 slice-done
  246.6 2.8 copy.64
  249.4 7.8 %copy.58 = f32[768,4,512]{0,2,1:T(8,128)} copy(f32[768,4,512]{2,1,0:T(4,128)} %slice.57) | data formatting | bytes 12582912 | tf_op jit(solution)/shard_map/reshape | solution.py:603
  257.2 0.0 copy-done
  257.2 7.3 %pad_maximum_fusion = f32[768,4,4,192]{0,3,2,1:T(8,128)} fusion(f32[768,4,4,64]{0,3,2,1:T(8,128)S(1)} %bitcast.52, f32[768,4,4,128]{0,3,2,1:T(8,128)} %bitcast.51), kind=kLoop, calls=%fused_computation | loop fusion | flops 2359296 | bytes 18874368 | tf_op jit(solution)/shard_map/concatenate | solution.py:605
  264.5 9.7 %copy.53 = f32[768,3072]{1,0:T(8,128)} copy(f32[768,3072]{0,1:T(8,128)} %bitcast.50) | data formatting | bytes 18874368
  274.2 0.0 reduce-scatter.14.cloned.1.call-update
  274.2 0.0 reduce-scatter.10.cloned.1.call-start
  274.3 12.9 %bitcast_convert_fusion = f32[4,768,1536]{2,1,0:T(8,128)} fusion(bf16[4,4,2,96,1536]{4,3,2,1,0:T(8,128)(2,1)} %get-tuple-element.42), kind=kLoop, calls=%fused_computation.1 | loop fusion | flops 4718592 | bytes 28311552 | tf_op jit(solution)/shard_map/reshape | solution.py:602
  287.1 0.0 reduce-scatter.10.cloned.1.call-update
  287.2 0.2 reduce-scatter.8.cloned.1.call-start
  287.4 79.7 %reduce-scatter.14.cloned.1.call-done = f32[96,3072]{1,0:T(8,128)} async-done(((f32[768,3072]{1,0:T(8,128)}), f32[96,3072]{1,0:T(8,128)}) %reduce-scatter.14.cloned.1.call-update) | async-done | bytes 1179664
  367.1 2.9 copy.54
  370.0 0.0 reduce-scatter.8.cloned.1.call-update
  370.1 3.8 copy.68
  373.9 0.5 broadcast
  374.4 11.6 %reduce = bf16[1024,768]{1,0:T(8,128)(2,1)} reduce(bf16[1024,1,768]{2,1,0:T(2,128)(2,1)S(1)} %bitcast.53, bf16[]{:T(256)} %broadcast), dimensions={1}, to_apply=%bitcast.49.reduce_sub_computation | reduce | bytes 3145730
  386.0 3.9 reshape.69
  389.9 4.6 all-to-all-start
  394.5 0.0 reduce-scatter.12.cloned.1.call-start
  394.5 102.4 %reduce-scatter.10.cloned.1.call-done = f32[4,96,1536]{2,1,0:T(8,128)} async-done(((f32[4,768,1536]{2,1,0:T(8,128)}), f32[4,96,1536]{2,1,0:T(8,128)}) %reduce-scatter.10.cloned.1.call-update) | async-done | bytes 2359312 | tf_op jit(solution)/shard_map/reduce_scatter | solution.py:623
  496.9 0.0 reduce-scatter.12.cloned.1.call-update
  496.9 3.8 copy.67
  500.7 11.6 %reduce.1 = bf16[1024,768]{1,0:T(8,128)(2,1)} reduce(bf16[1024,1,768]{2,1,0:T(2,128)(2,1)S(1)} %bitcast.54, bf16[]{:T(256)} %broadcast), dimensions={1}, to_apply=%bitcast.48.reduce_sub_computation | reduce | bytes 3145730
  512.4 3.7 reshape.67
  516.1 0.0 all-to-all-done
  516.1 4.6 all-to-all-start.1
  520.7 0.0 copy-done.2
  520.7 0.0 copy-done.3
  520.7 92.0 %all-reduce = f32[2,768]{1,0:T(2,128)S(1)} all-reduce(f32[2,768]{1,0:T(2,128)S(1)} %pad_maximum_fusion.6), channel_id=6, replica_groups=mesh['dp'=8,'tp'=4] {'dp','tp'}, use_global_device_ids=true, to_apply=%region_4.0.clone | all-reduce | flops 1536 | bytes 12288
  612.7 0.6 constant_dynamic-slice_fusion
  613.3 3.0 reshape.70
  616.4 1.4 copy.59
  617.8 0.0 all-to-all-done.1
  617.8 3.1 reshape.68
  620.8 1.9 copy.60
  622.7 1.0 slice_bitcast_fusion
  623.7 0.9 copy.52
  624.6 1.5 slice_bitcast_fusion.4
  626.1 1.8 slice_bitcast_fusion.1
  628.0 0.8 pad_maximum_fusion.1
  (9 shorter events, 0.0 us)
Async XLA Ops:
  7.2 7.6 %copy-start.4 = (f32[2,24]{1,0:T(2,128)S(1)}, f32[2,24]{1,0:T(2,128)}, u32[]{:S(2)}) copy-start(f32[2,24]{1,0:T(2,128)} %param.16) | copy-start | bytes 580
  7.2 359.9 %reduce-scatter.14.cloned.1.call-start = ((), (), s32[]{:S(2)}) async-start(), calls=%async_computation.9 | async-start | bytes 10616832
  15.1 0.6 copy-start.1
  239.9 6.7 %slice-start = ((f32[768,4,768]{2,1,0:T(4,128)}), f32[768,4,256]{2,1,0:T(4,128)S(1)}, s32[]{:S(2)}) async-start(f32[768,4,768]{2,1,0:T(4,128)} %reshape.60), calls=%async_computation.10 | async-start | bytes 6291456 | tf_op jit(solution)/shard_map/slice | solution.py:604
  249.4 7.8 %copy-start = (f32[768,4,256]{0,2,1:T(8,128)S(1)}, f32[768,4,256]{0,2,1:T(8,128)}, u32[]{:S(2)}) copy-start(f32[768,4,256]{0,2,1:T(8,128)} %copy.64) | copy-start | bytes 9437188
  274.2 222.7 %reduce-scatter.10.cloned.1.call-start = ((), (), s32[]{:S(2)}) async-start(), calls=%async_computation.7 | async-start | bytes 21233664 | tf_op jit(solution)/shard_map/reduce_scatter | solution.py:623
  287.2 335.5 %reduce-scatter.8.cloned.1.call-start = ((), (), s32[]{:S(2)}) async-start(), calls=%async_computation.6 | async-start | bytes 1966080 | tf_op jit(solution)/shard_map/reduce_scatter | solution.py:625
  389.9 126.3 %all-to-all-start = ((bf16[4,2,98304]{2,1,0:T(2,128)(2,1)}), bf16[4,2,98304]{2,1,0:T(2,128)(2,1)}, u32[]{:S(2)}, u32[]{:S(2)}) async-start(bf16[4,2,98304]{2,1,0:T(2,128)(2,1)} %reshape.69), calls=%async_computation | async-start | bytes 3145728 | tf_op jit(solution)/shard_map/all_to_all | solution.py:543
  394.5 231.6 %reduce-scatter.12.cloned.1.call-start = ((), (), s32[]{:S(2)}) async-start(), calls=%async_computation.8 | async-start | bytes 2949120 | tf_op jit(solution)/shard_map/reduce_scatter | solution.py:623
  512.4 8.3 %copy-start.2 = (f32[1,768]{1,0:T(1,128)S(1)}, f32[1,768]{1,0:T(1,128)}, u32[]{:S(2)}) copy-start(f32[1,768]{1,0:T(1,128)} %get-tuple-element.44) | copy-start | bytes 9220
  512.4 8.3 %copy-start.3 = (f32[1,768]{1,0:T(1,128)S(1)}, f32[1,768]{1,0:T(1,128)}, u32[]{:S(2)}) copy-start(f32[1,768]{1,0:T(1,128)} %get-tuple-element.43) | copy-start | bytes 9220
  516.1 101.7 %all-to-all-start.1 = ((bf16[4,2,98304]{2,1,0:T(2,128)(2,1)}), bf16[4,2,98304]{2,1,0:T(2,128)(2,1)}, u32[]{:S(2)}, u32[]{:S(2)}) async-start(bf16[4,2,98304]{2,1,0:T(2,128)(2,1)} %reshape.67), calls=%async_computation.1 | async-start | bytes 3145728 | tf_op jit(solution)/shard_map/all_to_all | solution.py:543
Sparse Core Ops, SparseCore 0:
  274.3 92.7 reduce-scatter.13
  370.7 126.1 reduce-scatter.9
  499.2 46.6 reduce-scatter.7
  548.1 55.3 reduce-scatter.11
